TPU v7x, 512 devices: a whole 4x8x8 slice. The times are simulated.
512 devices in a mesh: dp: 64 (over x, y, core), tensor: 8 (over z).
Axes of the slice: x: 4, y: 8, z: 8, core: 2. Of those that a mesh axis runs over, the one named last changes fastest.
Arguments:
- acts: bfloat16 [65536, 4096], P(('dp', 'tensor')), may hold values from -6 to 6
- grad_out: bfloat16 [65536, 1024], P('dp', 'tensor'), may hold values from -0.1875 to 0.1875
- error: bfloat16 [64, 4096, 1024], P('dp', None, 'tensor'), may hold values from -6 to 6
- q_init: float32 [1024, 32], P('tensor'), may hold values from -0.5 to 0.5
Outputs:
- new_error: bfloat16 [64, 4096, 1024], P('dp', None, 'tensor')
- q_factor: float32 [1024, 32], P('tensor')
- p_basis: float32 [8, 4096, 32], P('tensor')
All inputs are finite; a program needn't handle non-finite values.
Results may differ from a plain program's by a relative error of at most 0.00045.
Values may be sent and summed in bfloat16 or wider, within the bound.
A program may use at most 64 MiB of HBM per device.

v0:
```python
import jax
import jax.numpy as jnp
from jax import lax
from jax.sharding import PartitionSpec as P


def orthonormal(factor, gram):
    lower = jnp.linalg.cholesky(gram)
    return lax.linalg.triangular_solve(lower, factor, left_side=False, lower=True, transpose_a=True)


def per_device(acts, grad_out, error, q_init):
    grad = lax.dot_general(
        lax.all_gather(acts, "tensor", axis=0, tiled=True),
        grad_out,
        (((0,), (0,)), ((), ())),
        preferred_element_type=jnp.float32,
    )
    merged = grad + error[0].astype(jnp.float32)
    local_p = jnp.dot(merged, q_init, precision=lax.Precision.HIGHEST)
    total_p = lax.psum(local_p, "dp")
    gram = jnp.dot(total_p.T, total_p, precision=lax.Precision.HIGHEST)
    p_basis = orthonormal(total_p, gram)
    q_total = lax.psum(jnp.dot(merged.T, p_basis, precision=lax.Precision.HIGHEST), "dp")
    update = jnp.dot(p_basis, q_total.T, precision=lax.Precision.HIGHEST) / lax.axis_size("dp")
    new_error = (merged - update).astype(jnp.bfloat16)
    return (new_error[None], q_total, p_basis[None])


def solution(mesh):
    return jax.shard_map(
        per_device,
        mesh=mesh,
        in_specs=(
            P(("dp", "tensor"), None),
            P("dp", "tensor"),
            P("dp", None, "tensor"),
            P("tensor", None),
        ),
        out_specs=(P("dp", None, "tensor"), P("tensor", None), P("tensor", None, None)),
        check_vma=False,
    )
```

profile of v0, /device:TPU:1, one launch (start us, length us, event | category | flops | bytes accessed | tf_op | source)
XLA Modules:
  0.0 578.1 jit_solution(7843605813431726860)
XLA Ops:
  7.2 0.0 copy-start
  7.2 0.0 all-gather.2.cloned.1.call-start
  7.2 0.7 all-gather.2.cloned.1.call-update
  7.9 0.0 copy-start.3
  7.9 0.0 all-reduce.2.cloned.1.call-start
  8.0 105.2 %all-gather.2.cloned.1.call-done = bf16[1024,4096]{1,0:T(8,128)(2,1)} async-done(((bf16[128,4096]{1,0:T(8,128)(2,1)}), bf16[1024,4096]{1,0:T(8,128)(2,1)}) %all-gather.2.cloned.1.call-update) | async-done | bytes 8388624 | tf_op jit(solution)/shard_map/all_gather | solution.py:14
  113.2 0.0 copy-done
  113.2 6.0 %convolution_add_fusion = f32[4096,128]{1,0:T(8,128)S(1)} fusion(bf16[1024,4096]{1,0:T(8,128)(2,1)} %all-gather.2.cloned.1.call-done, bf16[1024,128]{1,0:T(8,128)(2,1)S(1)} %copy-done, bf16[1,4096,128]{2,1,0:T(8,128)(2,1)} %param.6), kind=kOutput, calls=%fused_computation.2 | convolution fusion | flops 1074790400 | bytes 11796480 | tf_op jit(solution)/shard_map/dot_general | solution.py:13
  119.2 0.0 copy-done.3
  119.2 3.0 fusion.7
  122.2 0.0 all-reduce.2.cloned.1.call-update
  122.2 189.3 %all-reduce.2.cloned.1.call-done = f32[4096,32]{0,1:T(8,128)} async-done(((f32[4096,32]{0,1:T(8,128)}), f32[4096,32]{0,1:T(8,128)}) %all-reduce.2.cloned.1.call-update) | async-done | bytes 524304 | tf_op jit(solution)/shard_map/psum | solution.py:21
  311.5 1.8 fusion.8
  313.3 0.1 copy.7
  313.4 2.9 cholesky.16
  316.3 0.6 compare_reduce_fusion
  317.0 0.7 fusion.3
  317.6 2.4 custom-call.6
  320.1 1.7 fusion.4
  321.8 0.0 copy-start.1
  321.8 1.3 fusion.9
  323.1 243.8 %psum.15 = f32[128,32]{0,1:T(8,128)S(1)} all-reduce(f32[128,32]{0,1:T(8,128)S(1)} %fusion.9), channel_id=1, replica_groups=mesh['dp'=64,'tensor'=8] {'dp'}, use_global_device_ids=true, to_apply=%region_3.4 | all-reduce | flops 4096 | bytes 32768 | tf_op jit(solution)/shard_map/psum | solution.py:24
  566.9 0.0 copy-start.2
  566.9 4.4 fusion.2
  571.3 0.0 copy-done.1
  571.3 0.0 copy-done.2
  (2 shorter events, 0.0 us)
Async XLA Ops:
  7.2 106.0 %copy-start = (bf16[1024,128]{1,0:T(8,128)(2,1)S(1)}, bf16[1024,128]{1,0:T(8,128)(2,1)}, u32[]{:S(2)}) copy-start(bf16[1024,128]{1,0:T(8,128)(2,1)} %param.5) | copy-start | bytes 786436
  7.2 106.0 %all-gather.2.cloned.1.call-start = ((), (), s32[]{:S(2)}) async-start(), calls=%async_computation | async-start | bytes 9437184 | tf_op jit(solution)/shard_map/all_gather | solution.py:14
  7.9 111.3 %copy-start.3 = (f32[128,32]{0,1:T(8,128)S(1)}, f32[128,32]{0,1:T(8,128)}, u32[]{:S(2)}) copy-start(f32[128,32]{0,1:T(8,128)} %param.7) | copy-start | bytes 49156
  7.9 303.6 %all-reduce.2.cloned.1.call-start = ((), (), s32[]{:S(2)}) async-start(), calls=%async_computation.1 | async-start | bytes 1048576 | tf_op jit(solution)/shard_map/psum | solution.py:21
  321.8 249.5 %copy-start.1 = (f32[4096,32]{0,1:T(8,128)}, f32[4096,32]{0,1:T(8,128)S(1)}, u32[]{:S(2)}) copy-start(f32[4096,32]{0,1:T(8,128)S(1)} %fusion.4) | copy-start | bytes 1572868
  566.9 4.4 copy-start.2
Sparse Core Ops, SparseCore 0:
  10.1 103.0 all-gather.1
  122.3 189.1 all-reduce.1
where the time goes:
time: 582 us; the launch traced here: 578 us
  waiting for transfers between devices  295 us (51%)
  blocking collectives  244 us (42%)
  matrix products  18.1 us (3%)
  between operations  14.1 us (2%)
  other arithmetic  6.69 us (1%)
    psum x1, blocking collectives, per_device(): lax.psum(jnp.dot(merged.T, p_basis, precision=lax.Precision.HIGHEST), 'dp')  244 us
    psum x1, waiting for transfers between devices, per_device(): total_p = lax.psum(local_p, 'dp')  189 us
    all_gather x1, waiting for transfers between devices, per_device(): lax.all_gather(acts, 'tensor', axis=0, tiled=True)  105 us
  transfers between devices with their start and end apart: 2, of which 2 were waited for; matrix products, arithmetic and copies ran while one was open for 0% of the time, Pallas kernels for 0%

commit v1 on v0

v1 whole, which is shorter than its diff:
```python
import jax
import jax.numpy as jnp
from jax import lax
from jax.experimental import pallas as pl
from jax.experimental.pallas import tpu as pltpu
from jax.sharding import PartitionSpec as P

NX, NY, NC, NZ = 4, 8, 2, 8
D, HEAD, RANK, TOK = 4096, 128, 32, 1024
BLOCK = TOK // NZ
CHUNKS = 8
WIDE = D // CHUNKS
HALF = WIDE // NC
ROWS_Y = HALF // NY
ROWS_X = ROWS_Y // NX
TILES = CHUNKS * RANK // HEAD
PER = CHUNKS // TILES
HIGHEST = lax.Precision.HIGHEST
MESH = pl.DeviceIdType.MESH


def dot(a, b, dims=((1,), (0,))):
    return lax.dot_general(a, b, (dims, ((), ())), precision=HIGHEST, preferred_element_type=jnp.float32)


def eliminate(gram, right):
    n = RANK
    row = lax.broadcasted_iota(jnp.int32, (n, n), 0)
    col = lax.broadcasted_iota(jnp.int32, (n, n), 1)
    left = jnp.concatenate([gram, jnp.where(row == col, 1.0, 0.0).astype(jnp.float32)], axis=1)
    rows = lax.broadcasted_iota(jnp.int32, (n, 1), 0)
    for j in range(n):
        inv = 1.0 / jnp.sqrt(left[j : j + 1, j : j + 1])
        pivot_l = left[j : j + 1, :] * inv
        pivot_r = right[j : j + 1, :] * inv
        factor = left[:, j : j + 1] * inv
        below = rows > j
        same = rows == j
        left = jnp.where(below, left - factor * pivot_l, jnp.where(same, pivot_l, left))
        right = jnp.where(below, right - factor * pivot_r, jnp.where(same, pivot_r, right))
    return left[:, n:], right


def kernel(
    acts, grad_out, error, q_init,
    new_error, q_out, p_out,
    abuf, gbuf, ebuf, merged, nbuf, core_in, core_sum, y_in, y_sum, x_in, own, pg, qcore, qy, qx,
    load_sem, g_sem, e_sem, out_sem, z_send, z_recv, c_send, c_recv, y_send, y_recv, x_send, x_recv,
    p_send, p_recv, q_send, q_recv,
):
    dp = lax.axis_index("dp")
    z = lax.axis_index("tensor")
    core = lax.rem(dp, NC)
    y = lax.rem(dp // NC, NY)
    x = dp // (NC * NY)

    def at(x_, y_, core_):
        return ((x_ * NY + y_) * NC + core_, z)

    up = (dp, lax.rem(z + 1, NZ))
    down = (dp, lax.rem(z + NZ - 1, NZ))
    sibling = at(x, y, 1 - core)
    ys = [(lax.rem(y + k, NY), at(x, lax.rem(y + k, NY), core)) for k in range(1, NY)]
    xs = [(lax.rem(x + k, NX), at(lax.rem(x + k, NX), y, core)) for k in range(1, NX)]

    def load(c):
        columns = pl.ds(pl.multiple_of(c * WIDE, WIDE), WIDE)
        return pltpu.make_async_copy(acts.at[:, columns], abuf.at[c, z], load_sem.at[c])

    @pl.loop(0, CHUNKS)
    def _(c):
        load(c).start()

    load_g = pltpu.make_async_copy(grad_out, gbuf, g_sem)
    load_e = pltpu.make_async_copy(error, ebuf, e_sem)
    load_g.start()
    load_e.start()

    barrier = pltpu.get_barrier_semaphore()
    partners = [up, down, sibling] + [d for _, d in ys] + [d for _, d in xs]
    for device in partners:
        pl.semaphore_signal(barrier, inc=1, device_id=device, device_id_type=MESH)
    pl.semaphore_wait(barrier, len(partners))

    def piece(c, slot, hop, way):
        if hop < 4:
            return abuf.at[c, slot]
        return abuf.at[c, slot, pl.ds(way * (BLOCK // 2), BLOCK // 2)]

    def z_copy(c, hop, way, sending):
        step = hop - 1 if sending else hop
        slot = lax.rem(z + (NZ - step if way == 0 else step), NZ)
        ref = piece(c, slot, hop, way)
        return pltpu.make_async_remote_copy(
            src_ref=ref, dst_ref=ref,
            send_sem=z_send.at[way, hop - 1, c], recv_sem=z_recv.at[way, hop - 1, c],
            device_id=up if way == 0 else down, device_id_type=MESH,
        )

    def to(ref_from, ref_to, send_sem, recv_sem, device):
        return pltpu.make_async_remote_copy(
            src_ref=ref_from, dst_ref=ref_to, send_sem=send_sem, recv_sem=recv_sem,
            device_id=device, device_id_type=MESH,
        )

    def wait_bytes(ref, sem):
        pltpu.make_async_copy(ref, ref, sem).wait()

    def rows_of(c, start, size):
        return pl.ds(pl.multiple_of(c * WIDE + start, 8), size)

    def core_copy(c):
        return to(
            merged.at[rows_of(c, (1 - core) * HALF, HALF)], core_in.at[c],
            c_send.at[c], c_recv.at[c], sibling,
        )

    def on(c, act):
        pl.when(jnp.logical_and(c >= 0, c < CHUNKS))(lambda: act(c))

    def own_send(c):
        load(c).wait()
        for way in range(2):
            z_copy(c, 1, way, True).start()

    def forward(hop):
        def act(c):
            for way in range(2):
                z_copy(c, hop, way, False).wait_recv()
                z_copy(c, hop + 1, way, True).start()
        return act

    def multiply(c):
        for way in range(2):
            z_copy(c, 4, way, False).wait_recv()
        grad = lax.dot_general(
            abuf[c].reshape(TOK, WIDE), gbuf[...], (((0,), (0,)), ((), ())),
            preferred_element_type=jnp.float32,
        )
        rows = rows_of(c, 0, WIDE)
        merged[rows, :] = grad + ebuf[rows, :].astype(jnp.float32)
        core_copy(c).start()

    def sum_core(c):
        core_copy(c).wait_recv()
        core_sum[c] = merged[rows_of(c, core * HALF, HALF), :] + core_in[c]
        for k, (other, device) in enumerate(ys):
            part = pl.ds(pl.multiple_of(other * ROWS_Y, ROWS_Y), ROWS_Y)
            to(core_sum.at[c, part], y_in.at[c, k], y_send.at[c], y_recv.at[c], device).start()

    def sum_y(c):
        wait_bytes(y_in.at[c], y_recv.at[c])
        total = core_sum[c, pl.ds(pl.multiple_of(y * ROWS_Y, ROWS_Y), ROWS_Y), :]
        for k in range(NY - 1):
            total = total + y_in[c, k]
        y_sum[c] = total
        for k, (other, device) in enumerate(xs):
            part = pl.ds(pl.multiple_of(other * ROWS_X, ROWS_X), ROWS_X)
            to(y_sum.at[c, part], x_in.at[c, k], x_send.at[c], x_recv.at[c], device).start()

    def sum_x(c):
        wait_bytes(x_in.at[c], x_recv.at[c])
        total = y_sum[c, pl.ds(pl.multiple_of(x * ROWS_X, ROWS_X), ROWS_X), :]
        for k in range(NX - 1):
            total = total + x_in[c, k]
        own[pl.ds(pl.multiple_of(c * ROWS_X, ROWS_X), ROWS_X), :] = total

    @pl.loop(0, CHUNKS + 6)
    def _(k):
        on(k, own_send)
        pl.when(k == 3)(lambda: (load_g.wait(), load_e.wait())[0])
        on(k - 1, forward(1))
        on(k - 5, sum_core)
        on(k - 2, forward(2))
        on(k - 6, sum_x)
        on(k - 3, forward(3))
        on(k - 5, sum_y)
        on(k - 4, multiply)

    m_own = own[...]
    p_own = dot(m_own, q_init[...])
    q_part = dot(p_own, m_own, ((0,), (0,)))
    qcore[0] = q_part
    q_c = to(qcore.at[0], qcore.at[1], q_send.at[0], q_recv.at[0], sibling)
    q_c.start()

    for t in range(TILES):
        pg[t, core, y, x] = jnp.concatenate(
            [p_own[(t * PER + j) * ROWS_X : (t * PER + j + 1) * ROWS_X, :] for j in range(PER)], axis=1
        )
        for _, device in xs:
            to(pg.at[t, core, y, x], pg.at[t, core, y, x], p_send.at[0, t], p_recv.at[0, t], device).start()

    q_c.wait_recv()
    qy[y] = qcore[0] + qcore[1]
    for _, device in ys:
        to(qy.at[y], qy.at[y], q_send.at[1], q_recv.at[1], device).start()

    for t in range(TILES):
        wait_bytes(pg.at[t, core, y, pl.ds(0, NX - 1)], p_recv.at[0, t])
        for _, device in ys:
            to(pg.at[t, core, y], pg.at[t, core, y], p_send.at[1, t], p_recv.at[1, t], device).start()

    wait_bytes(qy.at[pl.ds(0, NY - 1)], q_recv.at[1])
    total = qy[0]
    for k in range(1, NY):
        total = total + qy[k]
    qx[x] = total
    for _, device in xs:
        to(qx.at[x], qx.at[x], q_send.at[2], q_recv.at[2], device).start()

    for t in range(TILES):
        wait_bytes(pg.at[t, core, pl.ds(0, NY - 1)], p_recv.at[1, t])
        to(pg.at[t, core], pg.at[t, core], p_send.at[2, t], p_recv.at[2, t], sibling).start()

    wait_bytes(qx.at[pl.ds(0, NX - 1)], q_recv.at[2])
    q_t = qx[0]
    for k in range(1, NX):
        q_t = q_t + qx[k]

    gram = dot(q_t, q_init[...])
    inverse, q_fac = eliminate(gram, q_t)
    q_out[...] = q_fac
    back = dot(inverse, q_fac, ((0,), (0,))) * (1.0 / (NX * NY * NC))

    def spread(small):
        width = small.shape[1]
        tall = jnp.concatenate([small] * PER, axis=0)
        wide = jnp.concatenate([tall] * PER, axis=1)
        group_r = lax.broadcasted_iota(jnp.int32, wide.shape, 0) // RANK
        group_c = lax.broadcasted_iota(jnp.int32, wide.shape, 1) // width
        return jnp.where(group_r == group_c, wide, 0.0)

    to_basis = spread(inverse.T)
    to_update = spread(back)

    for t in range(TILES):
        to(pg.at[t, core], pg.at[t, 1 - core], p_send.at[2, t], p_recv.at[2, t], sibling).wait_recv()
        p_sum = pg[t].reshape(WIDE, HEAD)
        update = dot(p_sum, to_update)
        for j in range(PER):
            rows = pl.ds((t * PER + j) * WIDE, WIDE)
            nbuf[rows, :] = (merged[rows, :] - update[:, j * HEAD : (j + 1) * HEAD]).astype(jnp.bfloat16)
            pltpu.make_async_copy(nbuf.at[rows], new_error.at[rows], out_sem.at[t * PER + j]).start()
        p_out[t] = dot(p_sum, to_basis)

    @pl.loop(0, CHUNKS)
    def _(c):
        for way in range(2):
            for hop in range(1, 5):
                z_copy(c, hop, way, True).wait_send()
        core_copy(c).wait_send()
        wait_bytes(y_in.at[c], y_send.at[c])
        wait_bytes(x_in.at[c], x_send.at[c])
        rows = rows_of(c, 0, WIDE)
        pltpu.make_async_copy(nbuf.at[rows], new_error.at[rows], out_sem.at[c]).wait()
    for t in range(TILES):
        wait_bytes(pg.at[t, core, y, pl.ds(0, NX - 1)], p_send.at[0, t])
        wait_bytes(pg.at[t, core, pl.ds(0, NY - 1)], p_send.at[1, t])
        wait_bytes(pg.at[t, core], p_send.at[2, t])
    q_c.wait_send()
    wait_bytes(qy.at[pl.ds(0, NY - 1)], q_send.at[1])
    wait_bytes(qx.at[pl.ds(0, NX - 1)], q_send.at[2])


def per_device(acts, grad_out, error, q_init):
    f32, bf16 = jnp.float32, jnp.bfloat16
    dma = pltpu.SemaphoreType.DMA
    anywhere = pl.BlockSpec(memory_space=pl.ANY)
    vmem = pl.BlockSpec(memory_space=pltpu.VMEM)
    new_error, q_t, p_packed = pl.pallas_call(
        kernel,
        out_shape=(
            jax.ShapeDtypeStruct((D, HEAD), bf16),
            jax.ShapeDtypeStruct((RANK, HEAD), f32),
            jax.ShapeDtypeStruct((TILES, WIDE, HEAD), f32),
        ),
        in_specs=[anywhere, anywhere, anywhere, vmem],
        out_specs=(anywhere, vmem, vmem),
        scratch_shapes=[
            pltpu.VMEM((CHUNKS, NZ, BLOCK, WIDE), bf16),
            pltpu.VMEM((TOK, HEAD), bf16),
            pltpu.VMEM((D, HEAD), bf16),
            pltpu.VMEM((D, HEAD), f32),
            pltpu.VMEM((D, HEAD), bf16),
            pltpu.VMEM((CHUNKS, HALF, HEAD), f32),
            pltpu.VMEM((CHUNKS, HALF, HEAD), f32),
            pltpu.VMEM((CHUNKS, NY - 1, ROWS_Y, HEAD), f32),
            pltpu.VMEM((CHUNKS, ROWS_Y, HEAD), f32),
            pltpu.VMEM((CHUNKS, NX - 1, ROWS_X, HEAD), f32),
            pltpu.VMEM((CHUNKS * ROWS_X, HEAD), f32),
            pltpu.VMEM((TILES, NC, NY, NX, ROWS_X, HEAD), f32),
            pltpu.VMEM((2, RANK, HEAD), f32),
            pltpu.VMEM((NY, RANK, HEAD), f32),
            pltpu.VMEM((NX, RANK, HEAD), f32),
            dma((CHUNKS,)), dma, dma, dma((CHUNKS,)),
            dma((2, 4, CHUNKS)), dma((2, 4, CHUNKS)),
            dma((CHUNKS,)), dma((CHUNKS,)),
            dma((CHUNKS,)), dma((CHUNKS,)),
            dma((CHUNKS,)), dma((CHUNKS,)),
            dma((3, TILES)), dma((3, TILES)),
            dma((3,)), dma((3,)),
        ],
        compiler_params=pltpu.CompilerParams(
            collective_id=0, has_side_effects=True, vmem_limit_bytes=48 * 2**20
        ),
    )(acts, grad_out, error[0], q_init)
    p_basis = p_packed.reshape(TILES, WIDE, PER, RANK).transpose(0, 2, 1, 3).reshape(1, D, RANK)
    return new_error[None], q_t.T, p_basis


def solution(mesh):
    return jax.shard_map(
        per_device,
        mesh=mesh,
        in_specs=(
            P(("dp", "tensor"), None),
            P("dp", "tensor"),
            P("dp", None, "tensor"),
            P("tensor", None),
        ),
        out_specs=(P("dp", None, "tensor"), P("tensor", None), P("tensor", None, None)),
        check_vma=False,
    )
```

time: 582 us -> 150 us (0.26)
  waiting for transfers between devices: 295 us -> 0 us
  blocking collectives: 244 us -> 0 us
  Pallas kernels: 0 us -> 142 us
  matrix products: 18.1 us -> 0 us
  between operations: 14.1 us -> 0.67 us
  local copies, waits for them, and re-layouts: 0.1 us -> 7.47 us
  other arithmetic: 6.69 us -> 0 us
    psum x1 -> x0, blocking collectives: 244 us -> none  [per_device(): lax.psum(jnp.dot(merged.T, p_basis, precision=lax.Precision.HIGHEST), 'dp')]
    psum x1 -> x0, waiting for transfers between devices: 189 us -> none  [per_device(): total_p = lax.psum(local_p, 'dp')]
    pallas_call x0 -> x1, Pallas kernels: none -> 142 us  [per_device(): pl.pallas_call(kernel, out_shape=(jax.ShapeDtypeStruct((D, HEAD), bf16),...]
    all_gather x1 -> x0, waiting for transfers between devices: 105 us -> none  [per_device(): lax.all_gather(acts, 'tensor', axis=0, tiled=True)]
    dot_general x5 -> x0, matrix products: 16.4 us -> none  [the longest x1 5.99 us: per_device(): lax.dot_general(lax.all_gather(acts, 'tensor', axis=0, tiled=True), grad_...]
    another operation x5 -> x0, other arithmetic: 6.68 us -> none  [the longest x3 3.6 us: orthonormal(): lower = jnp.linalg.cholesky(gram)]
  transfers between devices with their start and end apart: 2 -> 0, of which waited for: 2 -> 0; matrix products, arithmetic and copies ran while one was open for 0% -> 0% of each run, Pallas kernels for 0% -> 0%
where the time goes in v1:
time: 150 us
  Pallas kernels  142 us (95%)
  local copies, waits for them, and re-layouts  7.47 us (5%)
    pallas_call x1, Pallas kernels, per_device(): pl.pallas_call(kernel, out_shape=(jax.ShapeDtypeStruct((D, HEAD), bf16),...  142 us
    unnamed x9, local copies, waits for them, and re-layouts  5.78 us

profile of v1, /device:TPU:1, one launch (start us, length us, event | category | flops | bytes accessed | tf_op | source)
XLA Modules:
  0.0 150.0 jit_solution(7327844656284998794)
XLA Ops:
  0.6 0.8 copy.11.q_init
  1.4 0.0 copy-start
  1.5 1.2 copy-done
  2.7 0.0 copy-start.1
  2.7 1.2 copy-done.1
  3.9 0.0 copy-start.2
  3.9 0.9 copy-done.2
  4.8 141.9 %shard_map.67 = (bf16[4096,128]{1,0:T(8,128)(2,1)S(1)}, f32[32,128]{1,0:T(8,128)S(1)}, f32[2,512,128]{2,1,0:T(8,128)S(1)}) custom-call(bf16[128,4096]{1,0:T(8,128)(2,1)S(1)} %copy-done, bf16[1024,128]{1,0:T(8,128)(2,1)S(1)} %copy-done.2, bf16[4096,128]{1,0:T(8,128)(2,1)S(1)} %bitcast.8, f32[128,32]{1,0:T(8,128)S(1)} %copy.11.q_init), custom_call_target="tpu_custom_call" | custom-call | tf_op jit(solution)/shard_map/pallas_call | solution.py:271
  146.8 0.2 copy.12
  147.0 0.3 copy.13
  147.3 1.2 reshape.13
  148.5 1.0 copy.16
  149.4 0.6 copy.17
Async XLA Ops:
  1.4 1.2 copy-start
  2.7 1.2 copy-start.1
  3.9 0.9 copy-start.2

commit v2 on v0

v2 whole, which is shorter than its diff:
```python
import jax
import jax.numpy as jnp
from jax import lax
from jax.experimental import pallas as pl
from jax.experimental.pallas import tpu as pltpu
from jax.sharding import PartitionSpec as P

NX, NY, NC, NZ = 4, 8, 2, 8
D, HEAD, RANK, TOK = 4096, 128, 32, 1024
BLOCK = TOK // NZ
CHUNKS = 8
WIDE = D // CHUNKS
LANES = WIDE // NX
PART = RANK // NC
F32, BF16 = jnp.float32, jnp.bfloat16
HIGHEST = lax.Precision.HIGHEST
MESH = pl.DeviceIdType.MESH
NT = ((1,), (1,))
NN = ((1,), (0,))
TN = ((0,), (0,))


def exact(a, b, dims=NN):
    return lax.dot_general(a, b, (dims, ((), ())), precision=HIGHEST, preferred_element_type=F32)


def single(a, b, dims=NN):
    return lax.dot_general(a, b, (dims, ((), ())), preferred_element_type=F32)


def split(value, parts):
    out = []
    for _ in range(parts):
        out.append(value.astype(BF16))
        value = value - out[-1].astype(F32)
    return out


def inverse_factor(gram):
    n = RANK
    row = lax.broadcasted_iota(jnp.int32, (n, n), 0)
    col = lax.broadcasted_iota(jnp.int32, (n, n), 1)
    both = jnp.concatenate([gram, jnp.where(row == col, 1.0, 0.0).astype(F32)], axis=1)
    rows = lax.broadcasted_iota(jnp.int32, (n, 1), 0)
    for j in range(n):
        inv = 1.0 / jnp.sqrt(both[j : j + 1, j : j + 1])
        pivot = both[j : j + 1, :] * inv
        factor = both[:, j : j + 1] * inv
        both = jnp.where(rows > j, both - factor * pivot, jnp.where(rows == j, pivot, both))
    return both[:, n:]


def kernel(
    acts, grad_out, error, q_init,
    new_error, q_out, p_out,
    abuf, gbuf, ebuf, qbuf, merged,
    w_out, w_in, w_split, partial, core_in, core_sum, x_in, x_sum, y_in, y_sum, z_in,
    pg, pt, pb, pb_rows, q_acc, q_core, qx_a, qy_a, qy_b, qx_b,
    load_sem, g_sem, e_sem, i_sem, z_send, z_recv, w_send, w_recv,
    c_send, c_recv, x_send, x_recv, y_send, y_recv, s_send, s_recv, p_send, p_recv, q_send, q_recv,
):
    dp = lax.axis_index("dp")
    z = lax.axis_index("tensor")
    core = lax.rem(dp, NC)
    y = lax.rem(dp // NC, NY)
    x = dp // (NC * NY)

    def at(x_, y_, core_):
        return ((x_ * NY + y_) * NC + core_, z)

    sibling = at(x, y, 1 - core)
    ys = [at(x, lax.rem(y + k, NY), core) for k in range(1, NY)]
    xs = [at(lax.rem(x + k, NX), y, core) for k in range(1, NX)]
    zs = [(dp, lax.rem(z + k, NZ)) for k in range(1, NZ)]
    up, down = zs[0], zs[-1]

    def to(ref_from, ref_to, send_sem, recv_sem, device):
        return pltpu.make_async_remote_copy(
            src_ref=ref_from, dst_ref=ref_to, send_sem=send_sem, recv_sem=recv_sem,
            device_id=device, device_id_type=MESH,
        )

    def wait_bytes(ref, sem):
        pltpu.make_async_copy(ref, ref, sem).wait()

    def load(c):
        columns = pl.ds(pl.multiple_of(c * WIDE, WIDE), WIDE)
        return pltpu.make_async_copy(acts.at[:, columns], abuf.at[c, z], load_sem.at[c])

    load_q = pltpu.make_async_copy(q_init, qbuf, i_sem)
    load_g = pltpu.make_async_copy(grad_out, gbuf, g_sem)
    load_e = pltpu.make_async_copy(error, ebuf, e_sem)
    load_q.start()
    load_g.start()

    @pl.loop(0, CHUNKS)
    def _(c):
        load(c).start()

    load_e.start()

    barrier = pltpu.get_barrier_semaphore()
    partners = [sibling] + ys + xs + zs
    for device in partners:
        pl.semaphore_signal(barrier, inc=1, device_id=device, device_id_type=MESH)

    load_q.wait()
    load_g.wait()
    q_parts = jnp.concatenate(split(qbuf[...], 3), axis=0)
    w_all = single(q_parts, gbuf[...], NT)
    w_all = w_all[:RANK] + w_all[RANK : 2 * RANK] + w_all[2 * RANK :]
    for s in range(NZ):
        for h in range(NC):
            w_out[s, h] = w_all[h * PART : (h + 1) * PART, s * BLOCK : (s + 1) * BLOCK]

    @pl.loop(0, CHUNKS)
    def _(c):
        load(c).wait()

    pl.semaphore_wait(barrier, len(partners))

    def w_copy(k):
        return to(w_out.at[lax.rem(z + k, NZ)], w_in.at[:, z], w_send.at[k - 1], w_recv, zs[k - 1])

    for k in range(1, NZ):
        w_copy(k).start()
    w_in[:, z] = w_out[z]

    def z_copy(c, hop, way, sending):
        step = hop - 1 if sending else hop
        slot = lax.rem(z + (NZ - step if way == 0 else step), NZ)
        ref = abuf.at[c, slot]
        if hop == 4:
            ref = abuf.at[c, slot, pl.ds(way * (BLOCK // 2), BLOCK // 2)]
        return to(ref, ref, z_send.at[way, hop - 1, c], z_recv.at[way, hop - 1, c], up if way == 0 else down)

    def on(c, act):
        pl.when(jnp.logical_and(c >= 0, c < CHUNKS))(lambda: act(c))

    def own_send(c):
        for way in range(2):
            z_copy(c, 1, way, True).start()

    def forward(hop):
        def act(c):
            for way in range(2):
                z_copy(c, hop, way, False).wait_recv()
                z_copy(c, hop + 1, way, True).start()
        return act

    def rows_of(c):
        return pl.ds(pl.multiple_of(c * WIDE, WIDE), WIDE)

    def multiply(c):
        for way in range(2):
            z_copy(c, 4, way, False).wait_recv()
        grad = single(abuf[c].reshape(TOK, WIDE), gbuf[...], TN)
        merged[rows_of(c), :] = grad + ebuf[rows_of(c), :].astype(F32)

    def w_ready():
        wait_bytes(w_in.at[:, pl.ds(0, NZ - 1)], w_recv)
        load_e.wait()
        w = w_in[...].reshape(NZ * RANK, BLOCK)
        for part, value in enumerate(split(w, 3)):
            w_split[part] = value

    def core_copy(i):
        return to(partial.at[i, 1 - core], core_in.at[i], c_send.at[i], c_recv.at[i], sibling)

    def p_partial(i):
        c = lax.rem(y + 1 + i, CHUNKS)
        a = abuf[c, z]
        total = single(w_split[0], a) + (single(w_split[1], a) + single(w_split[2], a))
        partial[i] = total.reshape(NC, NZ * PART, WIDE)
        e_all = single(jnp.concatenate(split(qbuf[...], 3), axis=0), ebuf[rows_of(c), :], NT)
        e_all = e_all[:RANK] + (e_all[RANK : 2 * RANK] + e_all[2 * RANK :])
        mine = pl.ds(pl.multiple_of(z * PART, PART), PART)
        for h in range(NC):
            partial[i, h, mine, :] = partial[i, h, mine, :] + e_all[h * PART : (h + 1) * PART]
        core_copy(i).start()

    def p_core(i):
        core_copy(i).wait_recv()
        total = partial[i, core] + core_in[i]
        for j in range(NX):
            core_sum[i, j] = total[:, j * LANES : (j + 1) * LANES]
        for k in range(1, NX):
            to(core_sum.at[i, lax.rem(x + k, NX)], x_in.at[i, k - 1], x_send.at[i], x_recv.at[i], xs[k - 1]).start()

    def y_copy(i):
        device = at(x, lax.rem(y + 1 + i, NY), core)
        return to(x_sum.at[i], y_in.at[i], y_send.at[i], y_recv, device)

    def p_x(i):
        wait_bytes(x_in.at[i], x_recv.at[i])
        total = core_sum[i, x]
        for k in range(NX - 1):
            total = total + x_in[i, k]
        x_sum[i] = total
        pl.when(i < CHUNKS - 1)(lambda: y_copy(i).start())

    def s_copy(k):
        return to(y_sum.at[lax.rem(z + k, NZ)], z_in.at[k - 1], s_send.at[k - 1], s_recv, zs[k - 1])

    def p_y():
        wait_bytes(y_in, y_recv)
        total = x_sum[CHUNKS - 1]
        for k in range(NY - 1):
            total = total + y_in[k]
        y_sum[...] = total.reshape(NZ, PART, LANES)
        for k in range(1, NZ):
            s_copy(k).start()

    def p_z():
        wait_bytes(z_in, s_recv)
        total = y_sum[z]
        for k in range(NZ - 1):
            total = total + z_in[k]
        mine = pg.at[core, y, x]
        mine[...] = total
        for device in xs:
            to(mine, mine, p_send.at[0], p_recv.at[0], device).start()

    def gather_y():
        wait_bytes(pg.at[core, y, pl.ds(0, NX - 1)], p_recv.at[0])
        for device in ys:
            to(pg.at[core, y], pg.at[core, y], p_send.at[1], p_recv.at[1], device).start()

    def gather_core():
        wait_bytes(pg.at[core, pl.ds(0, NY - 1)], p_recv.at[1])
        to(pg.at[core], pg.at[core], p_send.at[2], p_recv.at[2], sibling).start()

    def gather_done():
        wait_bytes(pg.at[core], p_recv.at[2])

        @pl.loop(0, CHUNKS)
        def _(c):
            for h in range(NC):
                for j in range(NX):
                    pt[c, h * PART : (h + 1) * PART, j * LANES : (j + 1) * LANES] = pg[h, c, j]

    def basis():
        tall = pt[...].reshape(CHUNKS * RANK, WIDE)
        square = exact(tall, tall, NT)
        gram = square[:RANK, :RANK]
        for c in range(1, CHUNKS):
            gram = gram + square[c * RANK : (c + 1) * RANK, c * RANK : (c + 1) * RANK]
        inverse = inverse_factor(gram)
        wide = jnp.concatenate([jnp.concatenate([inverse] * CHUNKS, axis=0)] * CHUNKS, axis=1)
        group_r = lax.broadcasted_iota(jnp.int32, wide.shape, 0) // RANK
        group_c = lax.broadcasted_iota(jnp.int32, wide.shape, 1) // RANK
        blocks = jnp.where(group_r == group_c, wide, 0.0)
        pb[...] = exact(blocks, tall).reshape(CHUNKS, RANK, WIDE)

    def basis_rows():
        @pl.loop(0, CHUNKS)
        def _(c):
            value = pb[c]
            p_out[:, rows_of(c)] = value
            high, low = [part.astype(F32) for part in split(value, 2)]
            stacked = jnp.concatenate([high, low, high, low], axis=0)
            pb_rows[rows_of(c), :] = stacked.T.astype(BF16)

        q_acc[...] = jnp.zeros_like(q_acc)

    def q_part(c):
        high, low = split(pb[c], 2)
        m_high, m_low = split(merged[rows_of(c), :], 2)
        first = single(jnp.concatenate([high, low], axis=0), m_high)
        q_acc[...] += first[:RANK] + (first[RANK:] + single(high, m_low))

    READY = 9

    def q_early(k):
        @pl.loop(0, READY - 4)
        def _(c):
            q_part(c)

    own_send(0)

    @pl.loop(0, CHUNKS + 4)
    def _(k):
        on(k + 1, own_send)
        pl.when(k == 1)(w_ready)
        on(2 * k - 2, p_partial)
        on(2 * k - 3, p_x)
        pl.when(k == 8)(gather_core)
        on(k - 1, forward(1))
        on(2 * k - 2, p_core)
        on(2 * k - 1, p_partial)
        pl.when(k == 7)(gather_y)
        pl.when(k == 8)(gather_done)
        on(k - 2, forward(2))
        on(2 * k - 1, p_core)
        pl.when(k == 8)(basis)
        on(k - 3, forward(3))
        on(2 * k - 2, p_x)
        pl.when(k == 5)(p_y)
        pl.when(k == 6)(p_z)
        pl.when(k == READY)(basis_rows)
        pl.when(k == READY)(lambda: q_early(k))
        on(k - 4, multiply)
        pl.when(k >= READY)(lambda: q_part(k - 4))

    q_core[0] = q_acc[...]
    q_c = to(q_core.at[0], q_core.at[1], q_send.at[0], q_recv.at[0], sibling)
    q_c.start()
    q_c.wait_recv()
    both = q_core[0] + q_core[1]

    def share(buf, place, value, sem, devices):
        buf[place] = value
        for device in devices:
            to(buf.at[place], buf.at[place], q_send.at[sem], q_recv.at[sem], device).start()

    def total_of(buf, sem):
        n = buf.shape[0]
        wait_bytes(buf.at[pl.ds(0, n - 1)], q_recv.at[sem])
        total = buf[0]
        for k in range(1, n):
            total = total + buf[k]
        return total

    share(qy_b, y, both[PART:], 2, ys)
    share(qx_a, x, both[:PART], 1, xs)
    share(qy_a, y, total_of(qx_a, 1), 3, ys)
    share(qx_b, x, total_of(qy_b, 2), 4, xs)
    q_t = jnp.concatenate([total_of(qy_a, 3), total_of(qx_b, 4)], axis=0)
    q_out[...] = q_t

    high, low = split(q_t * (1.0 / (NX * NY * NC)), 2)
    back = jnp.concatenate([high, high, low, low], axis=0)

    @pl.loop(0, CHUNKS)
    def _(c):
        update = single(pb_rows[rows_of(c), :], back)
        new_error[rows_of(c), :] = (merged[rows_of(c), :] - update).astype(BF16)

    @pl.loop(0, CHUNKS)
    def _(c):
        for way in range(2):
            for hop in range(1, 5):
                z_copy(c, hop, way, True).wait_send()
        core_copy(c).wait_send()
        wait_bytes(x_in.at[c], x_send.at[c])
        pl.when(c < CHUNKS - 1)(lambda: y_copy(c).wait_send())

    for k in range(1, NZ):
        w_copy(k).wait_send()
        s_copy(k).wait_send()
    wait_bytes(pg.at[core, y, pl.ds(0, NX - 1)], p_send.at[0])
    wait_bytes(pg.at[core, pl.ds(0, NY - 1)], p_send.at[1])
    wait_bytes(pg.at[core], p_send.at[2])
    q_c.wait_send()
    wait_bytes(qx_a.at[pl.ds(0, NX - 1)], q_send.at[1])
    wait_bytes(qy_b.at[pl.ds(0, NY - 1)], q_send.at[2])
    wait_bytes(qy_a.at[pl.ds(0, NY - 1)], q_send.at[3])
    wait_bytes(qx_b.at[pl.ds(0, NX - 1)], q_send.at[4])


def per_device(acts, grad_out, error, q_init):
    dma = pltpu.SemaphoreType.DMA
    hbm = pl.BlockSpec(memory_space=pltpu.HBM)
    vmem = pl.BlockSpec(memory_space=pltpu.VMEM)
    new_error, q_t, p_t = pl.pallas_call(
        kernel,
        out_shape=(
            jax.ShapeDtypeStruct((D, HEAD), BF16),
            jax.ShapeDtypeStruct((RANK, HEAD), F32),
            jax.ShapeDtypeStruct((RANK, D), F32),
        ),
        in_specs=[hbm, hbm, hbm, hbm],
        out_specs=(vmem, vmem, vmem),
        scratch_shapes=[
            pltpu.VMEM((CHUNKS, NZ, BLOCK, WIDE), BF16),
            pltpu.VMEM((TOK, HEAD), BF16),
            pltpu.VMEM((D, HEAD), BF16),
            pltpu.VMEM((RANK, HEAD), F32),
            pltpu.VMEM((D, HEAD), F32),
            pltpu.VMEM((NZ, NC, PART, BLOCK), F32),
            pltpu.VMEM((NC, NZ, PART, BLOCK), F32),
            pltpu.VMEM((3, NZ * RANK, BLOCK), BF16),
            pltpu.VMEM((CHUNKS, NC, NZ * PART, WIDE), F32),
            pltpu.VMEM((CHUNKS, NZ * PART, WIDE), F32),
            pltpu.VMEM((CHUNKS, NX, NZ * PART, LANES), F32),
            pltpu.VMEM((CHUNKS, NX - 1, NZ * PART, LANES), F32),
            pltpu.VMEM((CHUNKS, NZ * PART, LANES), F32),
            pltpu.VMEM((NY - 1, NZ * PART, LANES), F32),
            pltpu.VMEM((NZ, PART, LANES), F32),
            pltpu.VMEM((NZ - 1, PART, LANES), F32),
            pltpu.VMEM((NC, NY, NX, PART, LANES), F32),
            pltpu.VMEM((CHUNKS, RANK, WIDE), F32),
            pltpu.VMEM((CHUNKS, RANK, WIDE), F32),
            pltpu.VMEM((D, 4 * RANK), BF16),
            pltpu.VMEM((RANK, HEAD), F32),
            pltpu.VMEM((2, RANK, HEAD), F32),
            pltpu.VMEM((NX, PART, HEAD), F32),
            pltpu.VMEM((NY, PART, HEAD), F32),
            pltpu.VMEM((NY, PART, HEAD), F32),
            pltpu.VMEM((NX, PART, HEAD), F32),
            dma((CHUNKS,)), dma, dma, dma,
            dma((2, 4, CHUNKS)), dma((2, 4, CHUNKS)),
            dma((NZ - 1,)), dma,
            dma((CHUNKS,)), dma((CHUNKS,)),
            dma((CHUNKS,)), dma((CHUNKS,)),
            dma((CHUNKS,)), dma,
            dma((NZ - 1,)), dma,
            dma((3,)), dma((3,)),
            dma((5,)), dma((5,)),
        ],
        compiler_params=pltpu.CompilerParams(
            collective_id=0, has_side_effects=True, vmem_limit_bytes=56 * 2**20
        ),
    )(acts, grad_out, error[0], q_init.T)
    return new_error[None], q_t.T, p_t.T[None]


def solution(mesh):
    return jax.shard_map(
        per_device,
        mesh=mesh,
        in_specs=(
            P(("dp", "tensor"), None),
            P("dp", "tensor"),
            P("dp", None, "tensor"),
            P("tensor", None),
        ),
        out_specs=(P("dp", None, "tensor"), P("tensor", None), P("tensor", None, None)),
        check_vma=False,
    )
```

time: 582 us -> 120 us (0.21)
  waiting for transfers between devices: 295 us -> 0 us
  blocking collectives: 244 us -> 0 us
  Pallas kernels: 0 us -> 115 us
  matrix products: 18.1 us -> 0 us
  between operations: 14.1 us -> 0.66 us
  other arithmetic: 6.69 us -> 0 us
    psum x1 -> x0, blocking collectives: 244 us -> none  [per_device(): lax.psum(jnp.dot(merged.T, p_basis, precision=lax.Precision.HIGHEST), 'dp')]
    psum x1 -> x0, waiting for transfers between devices: 189 us -> none  [per_device(): total_p = lax.psum(local_p, 'dp')]
    pallas_call x0 -> x1, Pallas kernels: none -> 115 us  [per_device(): pl.pallas_call(kernel, out_shape=(jax.ShapeDtypeStruct((D, HEAD), BF16),...]
    all_gather x1 -> x0, waiting for transfers between devices: 105 us -> none  [per_device(): lax.all_gather(acts, 'tensor', axis=0, tiled=True)]
    dot_general x5 -> x0, matrix products: 16.4 us -> none  [the longest x1 5.99 us: per_device(): lax.dot_general(lax.all_gather(acts, 'tensor', axis=0, tiled=True), grad_...]
    another operation x5 -> x0, other arithmetic: 6.68 us -> none  [the longest x3 3.6 us: orthonormal(): lower = jnp.linalg.cholesky(gram)]
  transfers between devices with their start and end apart: 2 -> 0, of which waited for: 2 -> 0; matrix products, arithmetic and copies ran while one was open for 0% -> 0% of each run, Pallas kernels for 0% -> 0%
where the time goes in v2:
time: 120 us
  Pallas kernels  115 us (96%)
  local copies, waits for them, and re-layouts  3.73 us (3%)
    pallas_call x1, Pallas kernels, per_device(): pl.pallas_call(kernel, out_shape=(jax.ShapeDtypeStruct((D, HEAD), BF16),...  115 us
    unnamed x7, local copies, waits for them, and re-layouts  3.73 us

profile of v2, /device:TPU:1, one launch (start us, length us, event | category | flops | bytes accessed | tf_op | source)
XLA Modules:
  0.0 119.6 jit_solution(9752329526265046278)
XLA Ops:
  0.6 115.2 %shard_map.67 = (bf16[4096,128]{1,0:T(8,128)(2,1)}, f32[32,128]{1,0:T(8,128)}, f32[32,4096]{1,0:T(8,128)}) custom-call(bf16[128,4096]{1,0:T(8,128)(2,1)} %acts.1, bf16[1024,128]{1,0:T(8,128)(2,1)} %grad_out.1, bf16[4096,128]{1,0:T(8,128)(2,1)} %bitcast.7, f32[32,128]{1,0:T(8,128)} %bitcast.10), custom_call_target="tpu_custom_call" | custom-call | tf_op jit(solution)/shard_map/pallas_call | solution.py:365
  115.8 0.0 copy-start.1
  115.9 0.0 copy-start
  115.9 2.3 %copy.10 = bf16[1,4096,128]{2,1,0:T(8,128)(2,1)} copy(bf16[1,4096,128]{2,1,0:T(8,128)(2,1)} %bitcast.8) | data formatting | bytes 2097152
  118.2 0.0 copy-done.1
  118.2 0.6 copy.11
  118.8 0.0 copy-done
  118.8 0.8 copy.12
Async XLA Ops:
  115.8 2.3 %copy-start.1 = (f32[32,128]{1,0:T(8,128)S(1)}, f32[32,128]{1,0:T(8,128)}, u32[]{:S(2)}) copy-start(f32[32,128]{1,0:T(8,128)} %get-tuple-element.7) | copy-start | bytes 49156
  115.9 2.9 %copy-start = (f32[32,4096]{1,0:T(8,128)S(1)}, f32[32,4096]{1,0:T(8,128)}, u32[]{:S(2)}) copy-start(f32[32,4096]{1,0:T(8,128)} %get-tuple-element.8) | copy-start | bytes 1572868

commit v3 on v2

--- a/solution.py
+++ b/solution.py
@@ -9,6 +9,7 @@
 D, HEAD, RANK, TOK = 4096, 128, 32, 1024
 BLOCK = TOK // NZ
 CHUNKS = 8
+AHEAD = 2
 WIDE = D // CHUNKS
 LANES = WIDE // NX
 PART = RANK // NC
@@ -52,10 +53,10 @@
 
 def kernel(
     acts, grad_out, error, q_init,
-    new_error, q_out, p_out,
-    abuf, gbuf, ebuf, qbuf, merged,
+    merged, pb_rows, q_out, p_out,
+    abuf, gbuf, ebuf, qbuf,
     w_out, w_in, w_split, partial, core_in, core_sum, x_in, x_sum, y_in, y_sum, z_in,
-    pg, pt, pb, pb_rows, q_acc, q_core, qx_a, qy_a, qy_b, qx_b,
+    pg, pt, pb, small, q_acc, q_core, qx_a, qy_a, qy_b, qx_b,
     load_sem, g_sem, e_sem, i_sem, z_send, z_recv, w_send, w_recv,
     c_send, c_recv, x_send, x_recv, y_send, y_recv, s_send, s_recv, p_send, p_recv, q_send, q_recv,
 ):
@@ -104,6 +105,21 @@
     for device in partners:
         pl.semaphore_signal(barrier, inc=1, device_id=device, device_id_type=MESH)
 
+    def z_copy(c, hop, way, sending):
+        step = hop - 1 if sending else hop
+        slot = lax.rem(z + (NZ - step if way == 0 else step), NZ)
+        ref = abuf.at[c, slot]
+        if hop == 4:
+            ref = abuf.at[c, slot, pl.ds(way * (BLOCK // 2), BLOCK // 2)]
+        source = ref
+        if sending and hop == 1:
+            source = acts.at[:, pl.ds(pl.multiple_of(c * WIDE, WIDE), WIDE)]
+        return to(source, ref, z_send.at[way, hop - 1, c], z_recv.at[way, hop - 1, c], up if way == 0 else down)
+
+    def own_send(c):
+        for way in range(2):
+            z_copy(c, 1, way, True).start()
+
     load_q.wait()
     load_g.wait()
     q_parts = jnp.concatenate(split(qbuf[...], 3), axis=0)
@@ -113,33 +129,24 @@
         for h in range(NC):
             w_out[s, h] = w_all[h * PART : (h + 1) * PART, s * BLOCK : (s + 1) * BLOCK]
 
+    pl.semaphore_wait(barrier, len(partners))
+
+    def w_copy(k):
+        return to(w_out.at[lax.rem(z + k, NZ)], w_in.at[:, z], w_send.at[k - 1], w_recv, zs[k - 1])
+
+    for k in range(1, NZ):
+        w_copy(k).start()
+    w_in[:, z] = w_out[z]
+    for c in range(AHEAD):
+        own_send(c)
+
     @pl.loop(0, CHUNKS)
     def _(c):
         load(c).wait()
 
-    pl.semaphore_wait(barrier, len(partners))
-
-    def w_copy(k):
-        return to(w_out.at[lax.rem(z + k, NZ)], w_in.at[:, z], w_send.at[k - 1], w_recv, zs[k - 1])
-
-    for k in range(1, NZ):
-        w_copy(k).start()
-    w_in[:, z] = w_out[z]
-
-    def z_copy(c, hop, way, sending):
-        step = hop - 1 if sending else hop
-        slot = lax.rem(z + (NZ - step if way == 0 else step), NZ)
-        ref = abuf.at[c, slot]
-        if hop == 4:
-            ref = abuf.at[c, slot, pl.ds(way * (BLOCK // 2), BLOCK // 2)]
-        return to(ref, ref, z_send.at[way, hop - 1, c], z_recv.at[way, hop - 1, c], up if way == 0 else down)
 
     def on(c, act):
         pl.when(jnp.logical_and(c >= 0, c < CHUNKS))(lambda: act(c))
-
-    def own_send(c):
-        for way in range(2):
-            z_copy(c, 1, way, True).start()
 
     def forward(hop):
         def act(c):
@@ -239,18 +246,24 @@
                 for j in range(NX):
                     pt[c, h * PART : (h + 1) * PART, j * LANES : (j + 1) * LANES] = pg[h, c, j]
 
-    def basis():
+    def make_gram():
         tall = pt[...].reshape(CHUNKS * RANK, WIDE)
         square = exact(tall, tall, NT)
         gram = square[:RANK, :RANK]
         for c in range(1, CHUNKS):
             gram = gram + square[c * RANK : (c + 1) * RANK, c * RANK : (c + 1) * RANK]
-        inverse = inverse_factor(gram)
+        small[...] = gram
+
+    def make_inverse():
+        small[...] = inverse_factor(small[...])
+
+    def basis():
+        inverse = small[...]
         wide = jnp.concatenate([jnp.concatenate([inverse] * CHUNKS, axis=0)] * CHUNKS, axis=1)
         group_r = lax.broadcasted_iota(jnp.int32, wide.shape, 0) // RANK
         group_c = lax.broadcasted_iota(jnp.int32, wide.shape, 1) // RANK
         blocks = jnp.where(group_r == group_c, wide, 0.0)
-        pb[...] = exact(blocks, tall).reshape(CHUNKS, RANK, WIDE)
+        pb[...] = exact(blocks, pt[...].reshape(CHUNKS * RANK, WIDE)).reshape(CHUNKS, RANK, WIDE)
 
     def basis_rows():
         @pl.loop(0, CHUNKS)
@@ -269,38 +282,46 @@
         first = single(jnp.concatenate([high, low], axis=0), m_high)
         q_acc[...] += first[:RANK] + (first[RANK:] + single(high, m_low))
 
-    READY = 9
-
-    def q_early(k):
-        @pl.loop(0, READY - 4)
+    def q_early(start, end):
+        @pl.loop(start, end)
         def _(c):
             q_part(c)
 
-    own_send(0)
+    def when(k, tick, *acts_):
+        @pl.when(k == tick)
+        def _():
+            for act in acts_:
+                act()
 
     @pl.loop(0, CHUNKS + 4)
     def _(k):
-        on(k + 1, own_send)
-        pl.when(k == 1)(w_ready)
-        on(2 * k - 2, p_partial)
-        on(2 * k - 3, p_x)
-        pl.when(k == 8)(gather_core)
+        on(k + AHEAD, own_send)
+        step = 3 * k - 3
+        when(k, 1, w_ready)
+        on(step, p_partial)
+        on(step - 2, p_x)
+        when(k, 6, gather_y)
+        when(k, 7, gather_done)
+        when(k, 8, lambda: q_early(0, 3))
         on(k - 1, forward(1))
-        on(2 * k - 2, p_core)
-        on(2 * k - 1, p_partial)
-        pl.when(k == 7)(gather_y)
-        pl.when(k == 8)(gather_done)
+        on(step, p_core)
+        on(step + 1, p_partial)
+        on(step - 1, p_x)
+        when(k, 4, p_y)
+        when(k, 7, make_gram)
+        when(k, 8, lambda: q_early(3, 4))
         on(k - 2, forward(2))
-        on(2 * k - 1, p_core)
-        pl.when(k == 8)(basis)
+        on(step + 1, p_core)
+        on(step + 2, p_partial)
+        when(k, 5, p_z)
+        when(k, 7, make_inverse)
         on(k - 3, forward(3))
-        on(2 * k - 2, p_x)
-        pl.when(k == 5)(p_y)
-        pl.when(k == 6)(p_z)
-        pl.when(k == READY)(basis_rows)
-        pl.when(k == READY)(lambda: q_early(k))
+        on(step + 2, p_core)
+        on(step, p_x)
+        when(k, 6, gather_core)
+        when(k, 7, basis, basis_rows)
         on(k - 4, multiply)
-        pl.when(k >= READY)(lambda: q_part(k - 4))
+        pl.when(k >= 8)(lambda: q_part(k - 4))
 
     q_core[0] = q_acc[...]
     q_c = to(q_core.at[0], q_core.at[1], q_send.at[0], q_recv.at[0], sibling)
@@ -327,14 +348,6 @@
     share(qx_b, x, total_of(qy_b, 2), 4, xs)
     q_t = jnp.concatenate([total_of(qy_a, 3), total_of(qx_b, 4)], axis=0)
     q_out[...] = q_t
-
-    high, low = split(q_t * (1.0 / (NX * NY * NC)), 2)
-    back = jnp.concatenate([high, high, low, low], axis=0)
-
-    @pl.loop(0, CHUNKS)
-    def _(c):
-        update = single(pb_rows[rows_of(c), :], back)
-        new_error[rows_of(c), :] = (merged[rows_of(c), :] - update).astype(BF16)
 
     @pl.loop(0, CHUNKS)
     def _(c):
@@ -358,25 +371,51 @@
     wait_bytes(qx_b.at[pl.ds(0, NX - 1)], q_send.at[4])
 
 
+def update_kernel(merged, rows, q_t, p_t, new_error, q_out, p_out, buf, sems):
+    save_q = pltpu.make_async_copy(q_t, q_out, sems.at[CHUNKS])
+    save_p = pltpu.make_async_copy(p_t, p_out, sems.at[CHUNKS + 1])
+    save_q.start()
+    save_p.start()
+    high, low = split(q_t[...] * (1.0 / (NX * NY * NC)), 2)
+    back = jnp.concatenate([high, high, low, low], axis=0)
+
+    def save(c):
+        part = pl.ds(c * WIDE, WIDE)
+        return pltpu.make_async_copy(buf.at[part], new_error.at[part], sems.at[c])
+
+    for c in range(CHUNKS):
+        part = pl.ds(c * WIDE, WIDE)
+        buf[part, :] = (merged[part, :] - single(rows[part, :], back)).astype(BF16)
+        save(c).start()
+    for c in range(CHUNKS):
+        save(c).wait()
+    save_q.wait()
+    save_p.wait()
+
+
 def per_device(acts, grad_out, error, q_init):
     dma = pltpu.SemaphoreType.DMA
     hbm = pl.BlockSpec(memory_space=pltpu.HBM)
     vmem = pl.BlockSpec(memory_space=pltpu.VMEM)
-    new_error, q_t, p_t = pl.pallas_call(
+
+    def stay(array, place):
+        return pltpu.with_memory_space_constraint(array, place)
+
+    merged, rows, q_t, p_t = pl.pallas_call(
         kernel,
         out_shape=(
-            jax.ShapeDtypeStruct((D, HEAD), BF16),
-            jax.ShapeDtypeStruct((RANK, HEAD), F32),
-            jax.ShapeDtypeStruct((RANK, D), F32),
+            pltpu.VMEM((D, HEAD), F32),
+            pltpu.VMEM((D, 4 * RANK), BF16),
+            pltpu.VMEM((RANK, HEAD), F32),
+            pltpu.VMEM((RANK, D), F32),
         ),
-        in_specs=[hbm, hbm, hbm, hbm],
-        out_specs=(vmem, vmem, vmem),
+        in_specs=[hbm] * 4,
+        out_specs=(vmem,) * 4,
         scratch_shapes=[
             pltpu.VMEM((CHUNKS, NZ, BLOCK, WIDE), BF16),
             pltpu.VMEM((TOK, HEAD), BF16),
             pltpu.VMEM((D, HEAD), BF16),
             pltpu.VMEM((RANK, HEAD), F32),
-            pltpu.VMEM((D, HEAD), F32),
             pltpu.VMEM((NZ, NC, PART, BLOCK), F32),
             pltpu.VMEM((NC, NZ, PART, BLOCK), F32),
             pltpu.VMEM((3, NZ * RANK, BLOCK), BF16),
@@ -391,7 +430,7 @@
             pltpu.VMEM((NC, NY, NX, PART, LANES), F32),
             pltpu.VMEM((CHUNKS, RANK, WIDE), F32),
             pltpu.VMEM((CHUNKS, RANK, WIDE), F32),
-            pltpu.VMEM((D, 4 * RANK), BF16),
+            pltpu.VMEM((RANK, RANK), F32),
             pltpu.VMEM((RANK, HEAD), F32),
             pltpu.VMEM((2, RANK, HEAD), F32),
             pltpu.VMEM((NX, PART, HEAD), F32),
@@ -409,9 +448,21 @@
             dma((5,)), dma((5,)),
         ],
         compiler_params=pltpu.CompilerParams(
-            collective_id=0, has_side_effects=True, vmem_limit_bytes=56 * 2**20
+            collective_id=0, has_side_effects=True, vmem_limit_bytes=40 * 2**20
         ),
-    )(acts, grad_out, error[0], q_init.T)
+    )(*[stay(array, pltpu.HBM) for array in (acts, grad_out, error[0], q_init.T)])
+    new_error, q_t, p_t = pl.pallas_call(
+        update_kernel,
+        out_shape=(
+            jax.ShapeDtypeStruct((D, HEAD), BF16),
+            jax.ShapeDtypeStruct((RANK, HEAD), F32),
+            jax.ShapeDtypeStruct((RANK, D), F32),
+        ),
+        in_specs=[vmem] * 4,
+        out_specs=(hbm,) * 3,
+        scratch_shapes=[pltpu.VMEM((D, HEAD), BF16), dma((CHUNKS + 2,))],
+        compiler_params=pltpu.CompilerParams(vmem_limit_bytes=40 * 2**20),
+    )(*[stay(array, pltpu.VMEM) for array in (merged, rows, q_t, p_t)])
     return new_error[None], q_t.T, p_t.T[None]
 
 

time: 120 us -> 115 us (0.958)
  local copies, waits for them, and re-layouts: 3.73 us -> 0 us
    unnamed x7 -> x0, local copies, waits for them, and re-layouts: 3.73 us -> none
    pallas_call x1 -> x2, Pallas kernels: 115 us -> 114 us  [the longest x1 113 us: per_device(): pl.pallas_call(kernel, out_shape=(pltpu.VMEM((D, HEAD), F32), pltpu.VMEM(...]
where the time goes in v3:
time: 115 us
  Pallas kernels  114 us (99%)
    pallas_call x1, Pallas kernels, per_device(): pl.pallas_call(kernel, out_shape=(pltpu.VMEM((D, HEAD), F32), pltpu.VMEM(...  113 us

profile of v3, /device:TPU:1, one launch (start us, length us, event | category | flops | bytes accessed | tf_op | source)
XLA Modules:
  0.0 114.7 jit_solution(4243657524270068505)
XLA Ops:
  0.6 112.8 %shard_map.67 = (f32[4096,128]{1,0:T(8,128)S(1)}, bf16[4096,128]{1,0:T(8,128)(2,1)S(1)}, f32[32,128]{1,0:T(8,128)S(1)}, f32[32,4096]{1,0:T(8,128)S(1)}) custom-call(bf16[128,4096]{1,0:T(8,128)(2,1)} %acts.1, bf16[1024,128]{1,0:T(8,128)(2,1)} %grad_out.1, bf16[4096,128]{1,0:T(8,128)(2,1)} %bitcast.7, f32[32,128]{1,0:T(8,128)} %bitcast.8), custom_call_target="tpu_custom_call" | custom-call | tf_op jit(solution)/shard_map/pallas_call | solution.py:404
  113.5 1.3 %shard_map.68 = (bf16[4096,128]{1,0:T(8,128)(2,1)}, f32[32,128]{1,0:T(8,128)}, f32[32,4096]{1,0:T(8,128)}) custom-call(f32[4096,128]{1,0:T(8,128)S(1)} %get-tuple-element.10.merged, bf16[4096,128]{1,0:T(8,128)(2,1)S(1)} %get-tuple-element.11.rows, f32[32,128]{1,0:T(8,128)S(1)} %get-tuple-element.12.q_t, f32[32,4096]{1,0:T(8,128)S(1)} %get-tuple-element.13.p_t), custom_call_target="tpu_custom_call" | custom-call | tf_op jit(solution)/shard_map/pallas_call | solution.py:454

commit v4 on v3

--- a/solution.py
+++ b/solution.py
@@ -10,6 +10,7 @@
 BLOCK = TOK // NZ
 CHUNKS = 8
 AHEAD = 2
+FAR = NZ // 2
 WIDE = D // CHUNKS
 LANES = WIDE // NX
 PART = RANK // NC
@@ -56,9 +57,9 @@
     merged, pb_rows, q_out, p_out,
     abuf, gbuf, ebuf, qbuf,
     w_out, w_in, w_split, partial, core_in, core_sum, x_in, x_sum, y_in, y_sum, z_in,
-    pg, pt, pb, small, q_acc, q_core, qx_a, qy_a, qy_b, qx_b,
+    gperm, pg, pt, pb, small, u_out, u_in, q_acc, q_core, qx_a, qy_a, qy_b, qx_b,
     load_sem, g_sem, e_sem, i_sem, z_send, z_recv, w_send, w_recv,
-    c_send, c_recv, x_send, x_recv, y_send, y_recv, s_send, s_recv, p_send, p_recv, q_send, q_recv,
+    c_send, c_recv, x_send, x_recv, y_send, y_recv, s_send, s_recv, p_send, p_recv, u_send, u_recv, q_send, q_recv,
 ):
     dp = lax.axis_index("dp")
     z = lax.axis_index("tensor")
@@ -86,7 +87,7 @@
 
     def load(c):
         columns = pl.ds(pl.multiple_of(c * WIDE, WIDE), WIDE)
-        return pltpu.make_async_copy(acts.at[:, columns], abuf.at[c, z], load_sem.at[c])
+        return pltpu.make_async_copy(acts.at[:, columns], abuf.at[c, 0], load_sem.at[c])
 
     load_q = pltpu.make_async_copy(q_init, qbuf, i_sem)
     load_g = pltpu.make_async_copy(grad_out, gbuf, g_sem)
@@ -105,20 +106,21 @@
     for device in partners:
         pl.semaphore_signal(barrier, inc=1, device_id=device, device_id_type=MESH)
 
-    def z_copy(c, hop, way, sending):
-        step = hop - 1 if sending else hop
-        slot = lax.rem(z + (NZ - step if way == 0 else step), NZ)
-        ref = abuf.at[c, slot]
-        if hop == 4:
-            ref = abuf.at[c, slot, pl.ds(way * (BLOCK // 2), BLOCK // 2)]
-        source = ref
-        if sending and hop == 1:
-            source = acts.at[:, pl.ds(pl.multiple_of(c * WIDE, WIDE), WIDE)]
-        return to(source, ref, z_send.at[way, hop - 1, c], z_recv.at[way, hop - 1, c], up if way == 0 else down)
+    def slot_of(hop, way):
+        d = hop if way == 0 else (NZ - hop) % NZ
+        return NZ - 1 if d == FAR else d - (d > FAR)
+
+    def z_copy(c, hop, way):
+        source = abuf.at[c, slot_of(hop - 1, way)]
+        target = abuf.at[c, slot_of(hop, way)]
+        if hop == FAR:
+            part = pl.ds(way * (BLOCK // 2), BLOCK // 2)
+            source, target = source.at[part], target.at[part]
+        return to(source, target, z_send.at[way, hop - 1, c], z_recv.at[way, hop - 1, c], up if way == 0 else down)
 
     def own_send(c):
         for way in range(2):
-            z_copy(c, 1, way, True).start()
+            z_copy(c, 1, way).start()
 
     load_q.wait()
     load_g.wait()
@@ -129,6 +131,10 @@
         for h in range(NC):
             w_out[s, h] = w_all[h * PART : (h + 1) * PART, s * BLOCK : (s + 1) * BLOCK]
 
+    @pl.loop(0, CHUNKS)
+    def _(c):
+        load(c).wait()
+
     pl.semaphore_wait(barrier, len(partners))
 
     def w_copy(k):
@@ -140,9 +146,10 @@
     for c in range(AHEAD):
         own_send(c)
 
-    @pl.loop(0, CHUNKS)
-    def _(c):
-        load(c).wait()
+    for d in range(NZ):
+        rows = pl.ds(pl.multiple_of(lax.rem(z + NZ - d, NZ) * BLOCK, BLOCK), BLOCK)
+        place = NZ - 1 if d == FAR else d - (d > FAR)
+        gperm[place] = gbuf[rows, :]
 
 
     def on(c, act):
@@ -151,8 +158,8 @@
     def forward(hop):
         def act(c):
             for way in range(2):
-                z_copy(c, hop, way, False).wait_recv()
-                z_copy(c, hop + 1, way, True).start()
+                z_copy(c, hop, way).wait_recv()
+                z_copy(c, hop + 1, way).start()
         return act
 
     def rows_of(c):
@@ -160,9 +167,19 @@
 
     def multiply(c):
         for way in range(2):
-            z_copy(c, 4, way, False).wait_recv()
-        grad = single(abuf[c].reshape(TOK, WIDE), gbuf[...], TN)
+            z_copy(c, FAR - 1, way).wait_recv()
+        near = NZ - 1
+        grad = single(abuf[c, :near].reshape(near * BLOCK, WIDE), gperm[:near].reshape(near * BLOCK, HEAD), TN)
         merged[rows_of(c), :] = grad + ebuf[rows_of(c), :].astype(F32)
+
+    def far_send(c):
+        for way in range(2):
+            z_copy(c, FAR, way).start()
+
+    def finish(c):
+        for way in range(2):
+            z_copy(c, FAR, way).wait_recv()
+        merged[rows_of(c), :] += single(abuf[c, NZ - 1], gperm[NZ - 1], TN)
 
     def w_ready():
         wait_bytes(w_in.at[:, pl.ds(0, NZ - 1)], w_recv)
@@ -176,7 +193,7 @@
 
     def p_partial(i):
         c = lax.rem(y + 1 + i, CHUNKS)
-        a = abuf[c, z]
+        a = abuf[c, 0]
         total = single(w_split[0], a) + (single(w_split[1], a) + single(w_split[2], a))
         partial[i] = total.reshape(NC, NZ * PART, WIDE)
         e_all = single(jnp.concatenate(split(qbuf[...], 3), axis=0), ebuf[rows_of(c), :], NT)
@@ -206,8 +223,8 @@
         x_sum[i] = total
         pl.when(i < CHUNKS - 1)(lambda: y_copy(i).start())
 
-    def s_copy(k):
-        return to(y_sum.at[lax.rem(z + k, NZ)], z_in.at[k - 1], s_send.at[k - 1], s_recv, zs[k - 1])
+    def s_copy(k, w):
+        return to(y_sum.at[lax.rem(z + k + FAR * w, NZ)], z_in.at[w, k - 1], s_send.at[w, k - 1], s_recv.at[w], zs[k - 1])
 
     def p_y():
         wait_bytes(y_in, y_recv)
@@ -216,38 +233,65 @@
             total = total + y_in[k]
         y_sum[...] = total.reshape(NZ, PART, LANES)
         for k in range(1, NZ):
-            s_copy(k).start()
+            for w in range(2):
+                s_copy(k, w).start()
 
     def p_z():
-        wait_bytes(z_in, s_recv)
-        total = y_sum[z]
-        for k in range(NZ - 1):
-            total = total + z_in[k]
-        mine = pg.at[core, y, x]
-        mine[...] = total
-        for device in xs:
-            to(mine, mine, p_send.at[0], p_recv.at[0], device).start()
-
-    def gather_y():
-        wait_bytes(pg.at[core, y, pl.ds(0, NX - 1)], p_recv.at[0])
-        for device in ys:
-            to(pg.at[core, y], pg.at[core, y], p_send.at[1], p_recv.at[1], device).start()
+        for w in range(2):
+            wait_bytes(z_in.at[w], s_recv.at[w])
+            total = y_sum[lax.rem(z + FAR * w, NZ)]
+            for k in range(NZ - 1):
+                total = total + z_in[w, k]
+            mine = pg.at[w, core, x, y]
+            mine[...] = total
+            for device in ys:
+                to(mine, mine, p_send.at[0, w], p_recv.at[0, w], device).start()
+
+    def gather_x():
+        for w in range(2):
+            wait_bytes(pg.at[w, core, x, pl.ds(0, NY - 1)], p_recv.at[0, w])
+            mine = pg.at[w, core, x]
+            for device in xs:
+                to(mine, mine, p_send.at[1, w], p_recv.at[1, w], device).start()
 
     def gather_core():
-        wait_bytes(pg.at[core, pl.ds(0, NY - 1)], p_recv.at[1])
-        to(pg.at[core], pg.at[core], p_send.at[2], p_recv.at[2], sibling).start()
+        for w in range(2):
+            wait_bytes(pg.at[w, core, pl.ds(0, NX - 1)], p_recv.at[1, w])
+            to(pg.at[w, core], pg.at[w, core], p_send.at[2, w], p_recv.at[2, w], sibling).start()
 
     def gather_done():
-        wait_bytes(pg.at[core], p_recv.at[2])
+        for w in range(2):
+            wait_bytes(pg.at[w, core], p_recv.at[2, w])
 
         @pl.loop(0, CHUNKS)
         def _(c):
-            for h in range(NC):
-                for j in range(NX):
-                    pt[c, h * PART : (h + 1) * PART, j * LANES : (j + 1) * LANES] = pg[h, c, j]
+            for w in range(2):
+                for h in range(NC):
+                    for j in range(NX):
+                        pt[w, c, h * PART : (h + 1) * PART, j * LANES : (j + 1) * LANES] = pg[w, h, j, c]
+
+    def u_copy():
+        return to(u_out, u_in, u_send, u_recv, zs[FAR - 1])
+
+    def three(stacked):
+        return stacked[:RANK] + (stacked[RANK : 2 * RANK] + stacked[2 * RANK :])
+
+    def u_make():
+        u_out[...] = jnp.zeros_like(u_out)
+
+        @pl.loop(0, CHUNKS)
+        def _(c):
+            u_out[...] += three(single(jnp.concatenate(split(pt[1, c], 3), axis=0), abuf[c, 0], NT))
+
+        u_copy().start()
+
+    def u_use():
+        u_copy().wait_recv()
+        far = three(single(jnp.concatenate(split(u_in[...], 3), axis=0), gperm[NZ - 1]))
+        q_acc[...] += exact(small[...], far)
 
     def make_gram():
-        tall = pt[...].reshape(CHUNKS * RANK, WIDE)
+        tall = pt[0].reshape(CHUNKS * RANK, WIDE)
         square = exact(tall, tall, NT)
         gram = square[:RANK, :RANK]
         for c in range(1, CHUNKS):
@@ -263,7 +307,7 @@
         group_r = lax.broadcasted_iota(jnp.int32, wide.shape, 0) // RANK
         group_c = lax.broadcasted_iota(jnp.int32, wide.shape, 1) // RANK
         blocks = jnp.where(group_r == group_c, wide, 0.0)
-        pb[...] = exact(blocks, pt[...].reshape(CHUNKS * RANK, WIDE)).reshape(CHUNKS, RANK, WIDE)
+        pb[...] = exact(blocks, pt[0].reshape(CHUNKS * RANK, WIDE)).reshape(CHUNKS, RANK, WIDE)
 
     def basis_rows():
         @pl.loop(0, CHUNKS)
@@ -293,41 +337,43 @@
             for act in acts_:
                 act()
 
-    @pl.loop(0, CHUNKS + 4)
+    @pl.loop(0, CHUNKS + 3)
     def _(k):
         on(k + AHEAD, own_send)
         step = 3 * k - 3
         when(k, 1, w_ready)
         on(step, p_partial)
         on(step - 2, p_x)
-        when(k, 6, gather_y)
-        when(k, 7, gather_done)
-        when(k, 8, lambda: q_early(0, 3))
+        when(k, 8, basis, basis_rows)
+        when(k, 9, u_use)
         on(k - 1, forward(1))
         on(step, p_core)
         on(step + 1, p_partial)
         on(step - 1, p_x)
-        when(k, 4, p_y)
-        when(k, 7, make_gram)
-        when(k, 8, lambda: q_early(3, 4))
+        when(k, 6, gather_x)
+        when(k, 7, gather_core)
+        when(k, 8, lambda: q_early(0, 3))
         on(k - 2, forward(2))
+        when(k, 8, lambda: far_send(0), lambda: far_send(1))
+        when(k, 9, lambda: far_send(2), lambda: far_send(3), lambda: far_send(4), lambda: far_send(5))
         on(step + 1, p_core)
         on(step + 2, p_partial)
+        when(k, 4, p_y)
         when(k, 5, p_z)
-        when(k, 7, make_inverse)
-        on(k - 3, forward(3))
+        when(k, 7, gather_done, u_make, make_gram)
+        when(k, 8, lambda: q_early(3, 5))
+        on(k - 3, multiply)
         on(step + 2, p_core)
         on(step, p_x)
-        when(k, 6, gather_core)
-        when(k, 7, basis, basis_rows)
-        on(k - 4, multiply)
-        pl.when(k >= 8)(lambda: q_part(k - 4))
+        when(k, 7, make_inverse)
+        pl.when(k >= 8)(lambda: q_part(k - 3))
+
+    far_send(6)
+    far_send(7)
 
     q_core[0] = q_acc[...]
     q_c = to(q_core.at[0], q_core.at[1], q_send.at[0], q_recv.at[0], sibling)
     q_c.start()
-    q_c.wait_recv()
-    both = q_core[0] + q_core[1]
 
     def share(buf, place, value, sem, devices):
         buf[place] = value
@@ -342,28 +388,40 @@
             total = total + buf[k]
         return total
 
+    finish(0)
+    q_c.wait_recv()
+    both = q_core[0] + q_core[1]
     share(qy_b, y, both[PART:], 2, ys)
     share(qx_a, x, both[:PART], 1, xs)
+    finish(1)
+    finish(2)
     share(qy_a, y, total_of(qx_a, 1), 3, ys)
+    finish(3)
     share(qx_b, x, total_of(qy_b, 2), 4, xs)
-    q_t = jnp.concatenate([total_of(qy_a, 3), total_of(qx_b, 4)], axis=0)
-    q_out[...] = q_t
+    finish(4)
+    finish(5)
+    finish(6)
+    q_out[...] = jnp.concatenate([total_of(qy_a, 3), total_of(qx_b, 4)], axis=0)
+    finish(7)
 
     @pl.loop(0, CHUNKS)
     def _(c):
         for way in range(2):
             for hop in range(1, 5):
-                z_copy(c, hop, way, True).wait_send()
+                z_copy(c, hop, way).wait_send()
         core_copy(c).wait_send()
         wait_bytes(x_in.at[c], x_send.at[c])
         pl.when(c < CHUNKS - 1)(lambda: y_copy(c).wait_send())
 
     for k in range(1, NZ):
         w_copy(k).wait_send()
-        s_copy(k).wait_send()
-    wait_bytes(pg.at[core, y, pl.ds(0, NX - 1)], p_send.at[0])
-    wait_bytes(pg.at[core, pl.ds(0, NY - 1)], p_send.at[1])
-    wait_bytes(pg.at[core], p_send.at[2])
+        for w in range(2):
+            s_copy(k, w).wait_send()
+    for w in range(2):
+        wait_bytes(pg.at[w, core, x, pl.ds(0, NY - 1)], p_send.at[0, w])
+        wait_bytes(pg.at[w, core, pl.ds(0, NX - 1)], p_send.at[1, w])
+        wait_bytes(pg.at[w, core], p_send.at[2, w])
+    u_copy().wait_send()
     q_c.wait_send()
     wait_bytes(qx_a.at[pl.ds(0, NX - 1)], q_send.at[1])
     wait_bytes(qy_b.at[pl.ds(0, NY - 1)], q_send.at[2])
@@ -426,11 +484,14 @@
             pltpu.VMEM((CHUNKS, NZ * PART, LANES), F32),
             pltpu.VMEM((NY - 1, NZ * PART, LANES), F32),
             pltpu.VMEM((NZ, PART, LANES), F32),
-            pltpu.VMEM((NZ - 1, PART, LANES), F32),
-            pltpu.VMEM((NC, NY, NX, PART, LANES), F32),
-            pltpu.VMEM((CHUNKS, RANK, WIDE), F32),
+            pltpu.VMEM((2, NZ - 1, PART, LANES), F32),
+            pltpu.VMEM((NZ, BLOCK, HEAD), BF16),
+            pltpu.VMEM((2, NC, NX, NY, PART, LANES), F32),
+            pltpu.VMEM((2, CHUNKS, RANK, WIDE), F32),
             pltpu.VMEM((CHUNKS, RANK, WIDE), F32),
             pltpu.VMEM((RANK, RANK), F32),
+            pltpu.VMEM((RANK, BLOCK), F32),
+            pltpu.VMEM((RANK, BLOCK), F32),
             pltpu.VMEM((RANK, HEAD), F32),
             pltpu.VMEM((2, RANK, HEAD), F32),
             pltpu.VMEM((NX, PART, HEAD), F32),
@@ -443,8 +504,9 @@
             dma((CHUNKS,)), dma((CHUNKS,)),
             dma((CHUNKS,)), dma((CHUNKS,)),
             dma((CHUNKS,)), dma,
-            dma((NZ - 1,)), dma,
-            dma((3,)), dma((3,)),
+            dma((2, NZ - 1)), dma((2,)),
+            dma((3, 2)), dma((3, 2)),
+            dma, dma,
             dma((5,)), dma((5,)),
         ],
         compiler_params=pltpu.CompilerParams(

time: 115 us -> 110 us (0.957)
  Pallas kernels: 114 us -> 110 us
    pallas_call x1, Pallas kernels: 113 us -> 108 us  [per_device(): pl.pallas_call(kernel, out_shape=(pltpu.VMEM((D, HEAD), F32), pltpu.VMEM(...]
where the time goes in v4:
time: 110 us
  Pallas kernels  110 us (100%)
    pallas_call x1, Pallas kernels, per_device(): pl.pallas_call(kernel, out_shape=(pltpu.VMEM((D, HEAD), F32), pltpu.VMEM(...  108 us

profile of v4, /device:TPU:1, one launch (start us, length us, event | category | flops | bytes accessed | tf_op | source)
XLA Modules:
  0.0 110.3 jit_solution(15282620498216458671)
XLA Ops:
  0.6 108.4 %shard_map.67 = (f32[4096,128]{1,0:T(8,128)S(1)}, bf16[4096,128]{1,0:T(8,128)(2,1)S(1)}, f32[32,128]{1,0:T(8,128)S(1)}, f32[32,4096]{1,0:T(8,128)S(1)}) custom-call(bf16[128,4096]{1,0:T(8,128)(2,1)} %acts.1, bf16[1024,128]{1,0:T(8,128)(2,1)} %grad_out.1, bf16[4096,128]{1,0:T(8,128)(2,1)} %bitcast.7, f32[32,128]{1,0:T(8,128)} %bitcast.8), custom_call_target="tpu_custom_call" | custom-call | tf_op jit(solution)/shard_map/pallas_call | solution.py:462
  109.1 1.3 %shard_map.68 = (bf16[4096,128]{1,0:T(8,128)(2,1)}, f32[32,128]{1,0:T(8,128)}, f32[32,4096]{1,0:T(8,128)}) custom-call(f32[4096,128]{1,0:T(8,128)S(1)} %get-tuple-element.10.merged, bf16[4096,128]{1,0:T(8,128)(2,1)S(1)} %get-tuple-element.11.rows, f32[32,128]{1,0:T(8,128)S(1)} %get-tuple-element.12.q_t, f32[32,4096]{1,0:T(8,128)S(1)} %get-tuple-element.13.p_t), custom_call_target="tpu_custom_call" | custom-call | tf_op jit(solution)/shard_map/pallas_call | solution.py:516

commit v5 on v4

--- a/solution.py
+++ b/solution.py
@@ -116,7 +116,7 @@
         if hop == FAR:
             part = pl.ds(way * (BLOCK // 2), BLOCK // 2)
             source, target = source.at[part], target.at[part]
-        return to(source, target, z_send.at[way, hop - 1, c], z_recv.at[way, hop - 1, c], up if way == 0 else down)
+        return to(source, target, z_send.at[way, hop - 1], z_recv.at[way, hop - 1, c], up if way == 0 else down)
 
     def own_send(c):
         for way in range(2):
@@ -138,7 +138,7 @@
     pl.semaphore_wait(barrier, len(partners))
 
     def w_copy(k):
-        return to(w_out.at[lax.rem(z + k, NZ)], w_in.at[:, z], w_send.at[k - 1], w_recv, zs[k - 1])
+        return to(w_out.at[lax.rem(z + k, NZ)], w_in.at[:, z], w_send, w_recv, zs[k - 1])
 
     for k in range(1, NZ):
         w_copy(k).start()
@@ -189,7 +189,7 @@
             w_split[part] = value
 
     def core_copy(i):
-        return to(partial.at[i, 1 - core], core_in.at[i], c_send.at[i], c_recv.at[i], sibling)
+        return to(partial.at[i, 1 - core], core_in.at[i], c_send, c_recv.at[i], sibling)
 
     def p_partial(i):
         c = lax.rem(y + 1 + i, CHUNKS)
@@ -209,11 +209,11 @@
         for j in range(NX):
             core_sum[i, j] = total[:, j * LANES : (j + 1) * LANES]
         for k in range(1, NX):
-            to(core_sum.at[i, lax.rem(x + k, NX)], x_in.at[i, k - 1], x_send.at[i], x_recv.at[i], xs[k - 1]).start()
+            to(core_sum.at[i, lax.rem(x + k, NX)], x_in.at[i, k - 1], x_send, x_recv.at[i], xs[k - 1]).start()
 
     def y_copy(i):
         device = at(x, lax.rem(y + 1 + i, NY), core)
-        return to(x_sum.at[i], y_in.at[i], y_send.at[i], y_recv, device)
+        return to(x_sum.at[i], y_in.at[i], y_send, y_recv, device)
 
     def p_x(i):
         wait_bytes(x_in.at[i], x_recv.at[i])
@@ -224,7 +224,7 @@
         pl.when(i < CHUNKS - 1)(lambda: y_copy(i).start())
 
     def s_copy(k, w):
-        return to(y_sum.at[lax.rem(z + k + FAR * w, NZ)], z_in.at[w, k - 1], s_send.at[w, k - 1], s_recv.at[w], zs[k - 1])
+        return to(y_sum.at[lax.rem(z + k + FAR * w, NZ)], z_in.at[w, k - 1], s_send, s_recv.at[w], zs[k - 1])
 
     def p_y():
         wait_bytes(y_in, y_recv)
@@ -278,6 +278,7 @@
 
     def u_make():
         u_out[...] = jnp.zeros_like(u_out)
+        q_acc[...] = jnp.zeros_like(q_acc)
 
         @pl.loop(0, CHUNKS)
         def _(c):
@@ -287,8 +288,7 @@
 
     def u_use():
         u_copy().wait_recv()
-        far = three(single(jnp.concatenate(split(u_in[...], 3), axis=0), gperm[NZ - 1]))
-        q_acc[...] += exact(small[...], far)
+        q_acc[...] += three(single(jnp.concatenate(split(u_in[...], 3), axis=0), gperm[NZ - 1]))
 
     def make_gram():
         tall = pt[0].reshape(CHUNKS * RANK, WIDE)
@@ -318,13 +318,12 @@
             stacked = jnp.concatenate([high, low, high, low], axis=0)
             pb_rows[rows_of(c), :] = stacked.T.astype(BF16)
 
-        q_acc[...] = jnp.zeros_like(q_acc)
-
     def q_part(c):
-        high, low = split(pb[c], 2)
-        m_high, m_low = split(merged[rows_of(c), :], 2)
-        first = single(jnp.concatenate([high, low], axis=0), m_high)
-        q_acc[...] += first[:RANK] + (first[RANK:] + single(high, m_low))
+        a = split(pt[0, c], 3)
+        b = split(merged[rows_of(c), :], 3)
+        first = three(single(jnp.concatenate(a, axis=0), b[0]))
+        second = single(jnp.concatenate(a[:2], axis=0), b[1])
+        q_acc[...] += first + (second[:RANK] + (second[RANK:] + single(a[0], b[2])))
 
     def q_early(start, end):
         @pl.loop(start, end)
@@ -344,30 +343,25 @@
         when(k, 1, w_ready)
         on(step, p_partial)
         on(step - 2, p_x)
-        when(k, 8, basis, basis_rows)
-        when(k, 9, u_use)
         on(k - 1, forward(1))
         on(step, p_core)
         on(step + 1, p_partial)
         on(step - 1, p_x)
-        when(k, 6, gather_x)
-        when(k, 7, gather_core)
-        when(k, 8, lambda: q_early(0, 3))
+        when(k, 8, gather_core)
         on(k - 2, forward(2))
-        when(k, 8, lambda: far_send(0), lambda: far_send(1))
-        when(k, 9, lambda: far_send(2), lambda: far_send(3), lambda: far_send(4), lambda: far_send(5))
+        when(k, 9, *[lambda c=c: far_send(c) for c in range(6)])
         on(step + 1, p_core)
         on(step + 2, p_partial)
         when(k, 4, p_y)
         when(k, 5, p_z)
-        when(k, 7, gather_done, u_make, make_gram)
-        when(k, 8, lambda: q_early(3, 5))
+        when(k, 6, gather_x)
+        when(k, 8, gather_done, u_make, lambda: q_early(0, 5))
         on(k - 3, multiply)
         on(step + 2, p_core)
         on(step, p_x)
-        when(k, 7, make_inverse)
         pl.when(k >= 8)(lambda: q_part(k - 3))
 
+    u_use()
     far_send(6)
     far_send(7)
 
@@ -388,35 +382,31 @@
             total = total + buf[k]
         return total
 
-    finish(0)
+    make_gram()
     q_c.wait_recv()
     both = q_core[0] + q_core[1]
     share(qy_b, y, both[PART:], 2, ys)
     share(qx_a, x, both[:PART], 1, xs)
-    finish(1)
-    finish(2)
+    make_inverse()
     share(qy_a, y, total_of(qx_a, 1), 3, ys)
-    finish(3)
+    basis()
+    finish(0)
     share(qx_b, x, total_of(qy_b, 2), 4, xs)
-    finish(4)
-    finish(5)
-    finish(6)
-    q_out[...] = jnp.concatenate([total_of(qy_a, 3), total_of(qx_b, 4)], axis=0)
-    finish(7)
-
-    @pl.loop(0, CHUNKS)
-    def _(c):
-        for way in range(2):
-            for hop in range(1, 5):
-                z_copy(c, hop, way).wait_send()
-        core_copy(c).wait_send()
-        wait_bytes(x_in.at[c], x_send.at[c])
-        pl.when(c < CHUNKS - 1)(lambda: y_copy(c).wait_send())
-
-    for k in range(1, NZ):
-        w_copy(k).wait_send()
-        for w in range(2):
-            s_copy(k, w).wait_send()
+    basis_rows()
+    for c in range(1, CHUNKS - 1):
+        finish(c)
+    q_out[...] = exact(small[...], jnp.concatenate([total_of(qy_a, 3), total_of(qx_b, 4)], axis=0))
+    finish(CHUNKS - 1)
+
+    for way in range(2):
+        for hop in range(1, FAR):
+            wait_bytes(abuf.at[:, 0], z_send.at[way, hop - 1])
+        wait_bytes(abuf.at[:, 0, pl.ds(0, BLOCK // 2)], z_send.at[way, FAR - 1])
+    wait_bytes(w_in.at[:, pl.ds(0, NZ - 1)], w_send)
+    wait_bytes(core_in, c_send)
+    wait_bytes(x_in, x_send)
+    wait_bytes(y_in, y_send)
+    wait_bytes(z_in, s_send)
     for w in range(2):
         wait_bytes(pg.at[w, core, x, pl.ds(0, NY - 1)], p_send.at[0, w])
         wait_bytes(pg.at[w, core, pl.ds(0, NX - 1)], p_send.at[1, w])
@@ -499,12 +489,12 @@
             pltpu.VMEM((NY, PART, HEAD), F32),
             pltpu.VMEM((NX, PART, HEAD), F32),
             dma((CHUNKS,)), dma, dma, dma,
-            dma((2, 4, CHUNKS)), dma((2, 4, CHUNKS)),
-            dma((NZ - 1,)), dma,
-            dma((CHUNKS,)), dma((CHUNKS,)),
-            dma((CHUNKS,)), dma((CHUNKS,)),
-            dma((CHUNKS,)), dma,
-            dma((2, NZ - 1)), dma((2,)),
+            dma((2, FAR)), dma((2, FAR, CHUNKS)),
+            dma, dma,
+            dma, dma((CHUNKS,)),
+            dma, dma((CHUNKS,)),
+            dma, dma,
+            dma, dma((2,)),
             dma((3, 2)), dma((3, 2)),
             dma, dma,
             dma((5,)), dma((5,)),

time: 110 us -> 106 us (0.964)
  Pallas kernels: 110 us -> 105 us
    pallas_call x1, Pallas kernels: 108 us -> 104 us  [per_device(): pl.pallas_call(kernel, out_shape=(pltpu.VMEM((D, HEAD), F32), pltpu.VMEM(...]
where the time goes in v5:
time: 106 us
  Pallas kernels  105 us (99%)
    pallas_call x1, Pallas kernels, per_device(): pl.pallas_call(kernel, out_shape=(pltpu.VMEM((D, HEAD), F32), pltpu.VMEM(...  104 us

profile of v5, /device:TPU:1, one launch (start us, length us, event | category | flops | bytes accessed | tf_op | source)
XLA Modules:
  0.0 105.5 jit_solution(5038395335519771373)
XLA Ops:
  0.6 103.6 %shard_map.67 = (f32[4096,128]{1,0:T(8,128)S(1)}, bf16[4096,128]{1,0:T(8,128)(2,1)S(1)}, f32[32,128]{1,0:T(8,128)S(1)}, f32[32,4096]{1,0:T(8,128)S(1)}) custom-call(bf16[128,4096]{1,0:T(8,128)(2,1)} %acts.1, bf16[1024,128]{1,0:T(8,128)(2,1)} %grad_out.1, bf16[4096,128]{1,0:T(8,128)(2,1)} %bitcast.7, f32[32,128]{1,0:T(8,128)} %bitcast.8), custom_call_target="tpu_custom_call" | custom-call | tf_op jit(solution)/shard_map/pallas_call | solution.py:452
  104.2 1.3 %shard_map.68 = (bf16[4096,128]{1,0:T(8,128)(2,1)}, f32[32,128]{1,0:T(8,128)}, f32[32,4096]{1,0:T(8,128)}) custom-call(f32[4096,128]{1,0:T(8,128)S(1)} %get-tuple-element.10.merged, bf16[4096,128]{1,0:T(8,128)(2,1)S(1)} %get-tuple-element.11.rows, f32[32,128]{1,0:T(8,128)S(1)} %get-tuple-element.12.q_t, f32[32,4096]{1,0:T(8,128)S(1)} %get-tuple-element.13.p_t), custom_call_target="tpu_custom_call" | custom-call | tf_op jit(solution)/shard_map/pallas_call | solution.py:506

commit v6 on v5

--- a/solution.py
+++ b/solution.py
@@ -11,6 +11,7 @@
 CHUNKS = 8
 AHEAD = 2
 FAR = NZ // 2
+FAR_FIRST = (4, 3, 5, 2, 6, 1, 7)
 WIDE = D // CHUNKS
 LANES = WIDE // NX
 PART = RANK // NC
@@ -71,8 +72,8 @@
         return ((x_ * NY + y_) * NC + core_, z)
 
     sibling = at(x, y, 1 - core)
-    ys = [at(x, lax.rem(y + k, NY), core) for k in range(1, NY)]
-    xs = [at(lax.rem(x + k, NX), y, core) for k in range(1, NX)]
+    ys = [at(x, lax.rem(y + k, NY), core) for k in FAR_FIRST]
+    xs = [at(lax.rem(x + k, NX), y, core) for k in (2, 1, 3)]
     zs = [(dp, lax.rem(z + k, NZ)) for k in range(1, NZ)]
     up, down = zs[0], zs[-1]
 
@@ -85,6 +86,11 @@
     def wait_bytes(ref, sem):
         pltpu.make_async_copy(ref, ref, sem).wait()
 
+    barrier = pltpu.get_barrier_semaphore()
+    partners = [zs[k - 1] for k in FAR_FIRST] + ys + xs + [sibling]
+    for device in partners:
+        pl.semaphore_signal(barrier, inc=1, device_id=device, device_id_type=MESH)
+
     def load(c):
         columns = pl.ds(pl.multiple_of(c * WIDE, WIDE), WIDE)
         return pltpu.make_async_copy(acts.at[:, columns], abuf.at[c, 0], load_sem.at[c])
@@ -100,11 +106,6 @@
         load(c).start()
 
     load_e.start()
-
-    barrier = pltpu.get_barrier_semaphore()
-    partners = [sibling] + ys + xs + zs
-    for device in partners:
-        pl.semaphore_signal(barrier, inc=1, device_id=device, device_id_type=MESH)
 
     def slot_of(hop, way):
         d = hop if way == 0 else (NZ - hop) % NZ
@@ -140,7 +141,7 @@
     def w_copy(k):
         return to(w_out.at[lax.rem(z + k, NZ)], w_in.at[:, z], w_send, w_recv, zs[k - 1])
 
-    for k in range(1, NZ):
+    for k in FAR_FIRST:
         w_copy(k).start()
     w_in[:, z] = w_out[z]
     for c in range(AHEAD):
@@ -208,8 +209,8 @@
         total = partial[i, core] + core_in[i]
         for j in range(NX):
             core_sum[i, j] = total[:, j * LANES : (j + 1) * LANES]
-        for k in range(1, NX):
-            to(core_sum.at[i, lax.rem(x + k, NX)], x_in.at[i, k - 1], x_send, x_recv.at[i], xs[k - 1]).start()
+        for k, device in zip((2, 1, 3), xs):
+            to(core_sum.at[i, lax.rem(x + k, NX)], x_in.at[i, k - 1], x_send, x_recv.at[i], device).start()
 
     def y_copy(i):
         device = at(x, lax.rem(y + 1 + i, NY), core)
@@ -232,7 +233,7 @@
         for k in range(NY - 1):
             total = total + y_in[k]
         y_sum[...] = total.reshape(NZ, PART, LANES)
-        for k in range(1, NZ):
+        for k in FAR_FIRST:
             for w in range(2):
                 s_copy(k, w).start()
 
@@ -362,12 +363,11 @@
         pl.when(k >= 8)(lambda: q_part(k - 3))
 
     u_use()
-    far_send(6)
-    far_send(7)
-
     q_core[0] = q_acc[...]
     q_c = to(q_core.at[0], q_core.at[1], q_send.at[0], q_recv.at[0], sibling)
     q_c.start()
+    far_send(6)
+    far_send(7)
 
     def share(buf, place, value, sem, devices):
         buf[place] = value

time: 106 us -> 105 us (level)
  no operation moved by 1% of the time
where the time goes in v6:
time: 105 us
  Pallas kernels  104 us (99%)
    pallas_call x1, Pallas kernels, per_device(): pl.pallas_call(kernel, out_shape=(pltpu.VMEM((D, HEAD), F32), pltpu.VMEM(...  103 us

profile of v6, /device:TPU:1, one launch (start us, length us, event | category | flops | bytes accessed | tf_op | source)
XLA Modules:
  0.0 105.1 jit_solution(2281057253759166270)
XLA Ops:
  0.6 103.2 %shard_map.67 = (f32[4096,128]{1,0:T(8,128)S(1)}, bf16[4096,128]{1,0:T(8,128)(2,1)S(1)}, f32[32,128]{1,0:T(8,128)S(1)}, f32[32,4096]{1,0:T(8,128)S(1)}) custom-call(bf16[128,4096]{1,0:T(8,128)(2,1)} %acts.1, bf16[1024,128]{1,0:T(8,128)(2,1)} %grad_out.1, bf16[4096,128]{1,0:T(8,128)(2,1)} %bitcast.7, f32[32,128]{1,0:T(8,128)} %bitcast.8), custom_call_target="tpu_custom_call" | custom-call | tf_op jit(solution)/shard_map/pallas_call | solution.py:452
  103.8 1.3 %shard_map.68 = (bf16[4096,128]{1,0:T(8,128)(2,1)}, f32[32,128]{1,0:T(8,128)}, f32[32,4096]{1,0:T(8,128)}) custom-call(f32[4096,128]{1,0:T(8,128)S(1)} %get-tuple-element.10.merged, bf16[4096,128]{1,0:T(8,128)(2,1)S(1)} %get-tuple-element.11.rows, f32[32,128]{1,0:T(8,128)S(1)} %get-tuple-element.12.q_t, f32[32,4096]{1,0:T(8,128)S(1)} %get-tuple-element.13.p_t), custom_call_target="tpu_custom_call" | custom-call | tf_op jit(solution)/shard_map/pallas_call | solution.py:506

commit v7 on v6

--- a/solution.py
+++ b/solution.py
@@ -235,10 +235,10 @@
         y_sum[...] = total.reshape(NZ, PART, LANES)
         for k in FAR_FIRST:
             for w in range(2):
-                s_copy(k, w).start()
+                s_copy(k, 1 - w).start()
 
     def p_z():
-        for w in range(2):
+        for w in (1, 0):
             wait_bytes(z_in.at[w], s_recv.at[w])
             total = y_sum[lax.rem(z + FAR * w, NZ)]
             for k in range(NZ - 1):
@@ -249,27 +249,25 @@
                 to(mine, mine, p_send.at[0, w], p_recv.at[0, w], device).start()
 
     def gather_x():
-        for w in range(2):
+        for w in (1, 0):
             wait_bytes(pg.at[w, core, x, pl.ds(0, NY - 1)], p_recv.at[0, w])
             mine = pg.at[w, core, x]
             for device in xs:
                 to(mine, mine, p_send.at[1, w], p_recv.at[1, w], device).start()
 
     def gather_core():
-        for w in range(2):
+        for w in (1, 0):
             wait_bytes(pg.at[w, core, pl.ds(0, NX - 1)], p_recv.at[1, w])
             to(pg.at[w, core], pg.at[w, core], p_send.at[2, w], p_recv.at[2, w], sibling).start()
 
-    def gather_done():
-        for w in range(2):
-            wait_bytes(pg.at[w, core], p_recv.at[2, w])
+    def gather_done(w):
+        wait_bytes(pg.at[w, core], p_recv.at[2, w])
 
         @pl.loop(0, CHUNKS)
         def _(c):
-            for w in range(2):
-                for h in range(NC):
-                    for j in range(NX):
-                        pt[w, c, h * PART : (h + 1) * PART, j * LANES : (j + 1) * LANES] = pg[w, h, j, c]
+            for h in range(NC):
+                for j in range(NX):
+                    pt[w, c, h * PART : (h + 1) * PART, j * LANES : (j + 1) * LANES] = pg[w, h, j, c]
 
     def u_copy():
         return to(u_out, u_in, u_send, u_recv, zs[FAR - 1])
@@ -356,7 +354,7 @@
         when(k, 4, p_y)
         when(k, 5, p_z)
         when(k, 6, gather_x)
-        when(k, 8, gather_done, u_make, lambda: q_early(0, 5))
+        when(k, 8, lambda: gather_done(1), u_make, lambda: gather_done(0), lambda: q_early(0, 5))
         on(k - 3, multiply)
         on(step + 2, p_core)
         on(step, p_x)

time: 105 us -> 105 us (level)
  no operation moved by 1% of the time
where the time goes in v7:
time: 105 us
  Pallas kernels  104 us (99%)
    pallas_call x1, Pallas kernels, per_device(): pl.pallas_call(kernel, out_shape=(pltpu.VMEM((D, HEAD), F32), pltpu.VMEM(...  103 us

profile of v7, /device:TPU:1, one launch (start us, length us, event | category | flops | bytes accessed | tf_op | source)
XLA Modules:
  0.0 105.1 jit_solution(6192623452774037324)
XLA Ops:
  0.6 103.2 %shard_map.67 = (f32[4096,128]{1,0:T(8,128)S(1)}, bf16[4096,128]{1,0:T(8,128)(2,1)S(1)}, f32[32,128]{1,0:T(8,128)S(1)}, f32[32,4096]{1,0:T(8,128)S(1)}) custom-call(bf16[128,4096]{1,0:T(8,128)(2,1)} %acts.1, bf16[1024,128]{1,0:T(8,128)(2,1)} %grad_out.1, bf16[4096,128]{1,0:T(8,128)(2,1)} %bitcast.7, f32[32,128]{1,0:T(8,128)} %bitcast.8), custom_call_target="tpu_custom_call" | custom-call | tf_op jit(solution)/shard_map/pallas_call | solution.py:450
  103.8 1.3 %shard_map.68 = (bf16[4096,128]{1,0:T(8,128)(2,1)}, f32[32,128]{1,0:T(8,128)}, f32[32,4096]{1,0:T(8,128)}) custom-call(f32[4096,128]{1,0:T(8,128)S(1)} %get-tuple-element.10.merged, bf16[4096,128]{1,0:T(8,128)(2,1)S(1)} %get-tuple-element.11.rows, f32[32,128]{1,0:T(8,128)S(1)} %get-tuple-element.12.q_t, f32[32,4096]{1,0:T(8,128)S(1)} %get-tuple-element.13.p_t), custom_call_target="tpu_custom_call" | custom-call | tf_op jit(solution)/shard_map/pallas_call | solution.py:504
